TPU v7x, 128 devices: a whole 4x4x4 slice. The times are simulated.
128 devices in a mesh: sub: 32 (over z, x, core), lvl: 4 (over y).
Axes of the slice: x: 4, y: 4, z: 4, core: 2. Of those that a mesh axis runs over, the one named last changes fastest.
Arguments:
- vectors: bfloat16 [4096, 2, 256], P(('sub', 'lvl')), may hold values from -6 to 6
- self_blocks: bfloat16 [4096, 256, 256], P(('sub', 'lvl')), may hold values from -0.375 to 0.375
- near_blocks: bfloat16 [4096, 256, 256], P(('sub', 'lvl')), may hold values from -0.375 to 0.375
- near_row: int32 [4096], P(('sub', 'lvl')), may hold values from 0 to 31
- near_col: int32 [4096], P(('sub', 'lvl')), may hold values from 0 to 63
- bases: bfloat16 [4096, 256, 64], P(('sub', 'lvl')), may hold values from -0.375 to 0.375
- transfers: float32 [7936, 64, 64], P(('sub', 'lvl')), may hold values from -0.5 to 0.5
- far_row: int32 [16384], P(('sub', 'lvl')), may hold values from 0 to 31
- far_col: int32 [16384], P(('sub', 'lvl')), may hold values from 0 to 4095, as said below
- couplings: float32 [16384, 64, 64], P(('sub', 'lvl')), may hold values from -0.75 to 0.75
- root_couplings: float32 [128, 128, 64, 64], P(('sub', 'lvl')), may hold values from -1.5 to 1.5
Outputs:
- products: float32 [4096, 2, 256], P(('sub', 'lvl'))
Inputs may be any that keep to these rules, and one draw needn't show every extreme that they name: `far_col`: the column leaf of an admissible pair never lies on the owning device. Of each device's 128 pairs, exactly 16 have column leaves on each of the six devices 1, 2 or 3 places before or after it (cyclically over all devices). The others lie on devices more than 3 places away, at most 16 on any one device, and exactly 16 of them on one such device.
All inputs are finite; a program needn't handle non-finite values.
Results may differ from a plain program's by a relative error of at most 0.0024.
Values may be sent and summed in bfloat16 or wider, within the bound.
A program may use at most 128 MiB of HBM per device.

v0:
```python
import jax
import jax.numpy as jnp
from jax import lax
from jax.sharding import PartitionSpec as P

HIGH = lax.Precision.HIGHEST


def from_behind(x, axis, by):
    devices = lax.axis_size(axis)
    return lax.ppermute(x, axis, [(i, (i + by) % devices) for i in range(devices)])


def tree_levels(count):
    levels = []
    offset = 0
    width = count
    while width > 1:
        levels.append((offset, width))
        offset += width
        width //= 2
    return levels


def tree_up(coeff, trans):
    for offset, width in tree_levels(coeff.shape[0]):
        prod = jnp.einsum("nvk,nkr->nvr", coeff, trans[offset : offset + width], precision=HIGH)
        coeff = prod.reshape(width // 2, 2, 2, prod.shape[-1]).sum(axis=1)
    return coeff[0]


def tree_down(top, leaf_terms, trans):
    field = top[None]
    for offset, width in reversed(tree_levels(leaf_terms.shape[0])):
        field = jnp.einsum(
            "nkr,nvr->nvk",
            trans[offset : offset + width],
            jnp.repeat(field, 2, axis=0),
            precision=HIGH,
        )
    return field + leaf_terms


def one_hot(index, count):
    slots = lax.broadcasted_iota(jnp.int32, (count, index.shape[0]), 0)
    return (slots == index[None, :]).astype(jnp.float32)


def shards(
    vectors,
    self_blocks,
    near_blocks,
    near_row,
    near_col,
    bases,
    transfers,
    far_row,
    far_col,
    couplings,
    root_couplings,
):
    count = vectors.shape[0]
    rank = bases.shape[2]
    pairs = far_row.shape[0]
    devices = lax.axis_size(("sub", "lvl"))
    coeff = jnp.einsum("lvi,lik->lvk", vectors, bases, preferred_element_type=jnp.float32)
    flat = coeff.reshape(count, 2 * rank)
    root = tree_up(coeff, transfers)
    roots = lax.all_gather(root.reshape(1, 2 * rank), ("sub", "lvl"), axis=0, tiled=True)
    root_field = jnp.einsum(
        "erk,evk->vr", root_couplings[0], roots.reshape(devices, 2, rank), precision=HIGH
    )
    following = from_behind(vectors, ("sub", "lvl"), -1)
    both = jnp.concatenate([vectors, following], axis=0)
    forward = jnp.einsum(
        "pij,pvj->pvi", near_blocks, both[near_col], preferred_element_type=jnp.float32
    )
    backward = jnp.einsum(
        "pij,pvi->pvj", near_blocks, vectors[near_row], preferred_element_type=jnp.float32
    )
    self_out = jnp.einsum("lij,lvj->lvi", self_blocks, vectors, preferred_element_type=jnp.float32)
    near_own = jnp.einsum("lp,pvi->lvi", one_hot(near_row, count), forward, precision=HIGH)
    back_all = jnp.einsum("lp,pvj->lvj", one_hot(near_col, 2 * count), backward, precision=HIGH)
    returned = from_behind(back_all[count:], ("sub", "lvl"), 1)
    near_part = self_out + near_own + back_all[:count] + returned
    gathered = lax.all_gather(flat, ("sub", "lvl"), axis=0, tiled=True)
    partner = gathered[far_col]
    far_forward = jnp.einsum(
        "prk,pvk->pvr", couplings, partner.reshape(pairs, 2, rank), precision=HIGH
    )
    leaf_field = jnp.einsum("lp,pvr->lvr", one_hot(far_row, count), far_forward, precision=HIGH)
    far_backward = jnp.einsum("prk,pvr->pvk", couplings, coeff[far_row], precision=HIGH).reshape(
        pairs, 2 * rank
    )
    incoming = lax.psum_scatter(
        jnp.dot(
            one_hot(far_col, lax.axis_size(("sub", "lvl")) * count), far_backward, precision=HIGH
        ),
        ("sub", "lvl"),
        scatter_dimension=0,
        tiled=True,
    )
    leaf_field = leaf_field + incoming.reshape(count, 2, rank)
    field = tree_down(root_field, leaf_field, transfers).astype(jnp.bfloat16)
    far_part = jnp.einsum("lik,lvk->lvi", bases, field, preferred_element_type=jnp.float32)
    return near_part + far_part


def solution(mesh):
    in_specs = (
        P(("sub", "lvl"), None, None),
        P(("sub", "lvl"), None, None),
        P(("sub", "lvl"), None, None),
        P(("sub", "lvl")),
        P(("sub", "lvl")),
        P(("sub", "lvl"), None, None),
        P(("sub", "lvl"), None, None),
        P(("sub", "lvl")),
        P(("sub", "lvl")),
        P(("sub", "lvl"), None, None),
        P(("sub", "lvl"), None, None, None),
    )
    out_specs = P(("sub", "lvl"), None, None)
    return jax.shard_map(shards, mesh=mesh, in_specs=in_specs, out_specs=out_specs, check_vma=False)
```

profile of v0, /device:TPU:1, one launch (start us, length us, event | category | flops | bytes accessed | tf_op | source)
XLA Modules:
  0.0 726.6 jit_solution(6082238529405344043)
XLA Ops:
  6.5 1.8 fusion.49
  8.3 0.7 reshape.59
  9.1 4.2 collective-permute-start
  13.3 0.7 compare_select_fusion
  13.9 0.7 gather_fusion.3
  14.7 5.6 copy.33
  20.3 5.3 fusion.51
  25.7 2.4 fusion.2
  28.1 0.6 gather_fusion.1
  28.8 3.0 fusion.48
  32.3 1.0 bitcast_reduce_fusion
  34.7 52.1 %all-gather = f32[128,1,128]{2,1,0:T(1,128)S(1)} all-gather(f32[1,1,128]{2,1,0:T(1,128)S(1)} %reshape.99), channel_id=1, replica_groups=mesh['sub'=32,'lvl'=4] {'sub','lvl'}, dimensions={0}, use_global_device_ids=true | all-gather | bytes 66048 | tf_op jit(solution)/shard_map/all_gather | solution.py:69
  86.9 2.7 fusion.7
  89.6 1.0 fusion.33
  90.7 1.2 fusion.24
  91.9 1.5 fusion.18
  93.4 2.0 fusion.14
  96.1 3.4 fusion.47
  99.7 2.2 gather_fusion.2
  102.2 8.4 %fusion.50 = f32[128,2,64]{2,1,0:T(2,128)S(1)} fusion(f32[128,2,64]{2,1,0:T(2,128)S(1)} %copy.32, f32[128,64,64]{2,1,0:T(8,128)} %copy.33), kind=kOutput, calls=%fused_computation.70 | convolution fusion | flops 12582912 | bytes 2228224 | tf_op jit(solution)/shard_map/prk,pvk->pvr/dot_general | solution.py:88
  110.8 600.9 %reduce-scatter.2.cloned.1.call-done = f32[32,128]{1,0:T(8,128)} async-done(((f32[4096,128]{1,0:T(8,128)}), f32[32,128]{1,0:T(8,128)}) %reduce-scatter.2.cloned.1.call-update) | async-done | bytes 16400 | tf_op jit(solution)/shard_map/reduce_scatter | solution.py:95
  711.7 0.8 reshape.62
  712.5 3.0 fusion.6
  715.7 4.0 fusion.5
  (52 shorter events, 3.8 us)
Async XLA Ops:
  6.5 80.4 %copy-start = (f32[1,128,64,64]{1,3,2,0:T(8,128)S(1)}, f32[1,128,64,64]{1,3,2,0:T(8,128)}, u32[]{:S(2)}) copy-start(f32[1,128,64,64]{1,3,2,0:T(8,128)} %param.21) | copy-start | bytes 6291460
  6.5 93.2 %all-gather.3.cloned.1.call-start = ((), (), s32[]{:S(2)}) async-start(), calls=%async_computation.1 | async-start | bytes 2113536 | tf_op jit(solution)/shard_map/all_gather | solution.py:86
  9.0 702.6 %reduce-scatter.2.cloned.1.call-start = ((), (), s32[]{:S(2)}) async-start(), calls=%async_computation.2 | async-start | bytes 2113536 | tf_op jit(solution)/shard_map/reduce_scatter | solution.py:95
  9.1 86.3 %collective-permute-start = (bf16[32,2,256]{2,1,0:T(2,128)(2,1)}, bf16[32,2,256]{2,1,0:T(2,128)(2,1)S(1)}, u32[]{:S(2)}, u32[]{:S(2)}) collective-permute-start(bf16[32,2,256]{2,1,0:T(2,128)(2,1)} %param.11), channel_id=1, source_target_pairs={{0,127},{1,0},{2,1},{3,2},{4,3},{5,4},{6,5},{7,6},{8,7},{9,8},{10,... | collective-permute-start | bytes 98312 | tf_op jit(solution)/shard_map/ppermute | solution.py:11
  20.3 5.4 copy-start.4
  25.6 2.4 copy-start.6
  25.7 2.5 copy-start.3
  28.8 3.0 copy-start.5
  28.8 3.5 copy-start.1
  32.2 683.5 %collective-permute-start.1 = (f32[32,2,256]{2,1,0:T(2,128)S(1)}, f32[32,2,256]{2,1,0:T(2,128)}, u32[]{:S(2)}, u32[]{:S(2)}) collective-permute-start(f32[32,2,256]{2,1,0:T(2,128)S(1)} %copy.39), channel_id=1, source_target_pairs={{0,1},{1,2},{2,3},{3,4},{4,5},{5,6},{6,7},{7,8},{8,9},{9,10},{10,1... | collective-permute-start | bytes 196616 | tf_op jit(solution)/shard_map/ppermute | solution.py:11
  102.2 8.4 %copy-start.7 = (s32[128]{0:T(128)S(1)}, s32[128]{0:T(128)}, u32[]{:S(2)}) copy-start(s32[128]{0:T(128)} %param.18) | copy-start | bytes 1540
  102.2 613.3 %copy-start.2 = (bf16[32,256,64]{1,2,0:T(8,128)(2,1)S(1)}, bf16[32,256,64]{1,2,0:T(8,128)(2,1)}, u32[]{:S(2)}) copy-start(bf16[32,256,64]{1,2,0:T(8,128)(2,1)} %param.16) | copy-start | bytes 3145732
Sparse Core Ops, SparseCore 0:
  10.3 68.8 all-gather.2
  81.6 630.0 reduce-scatter.1
where the time goes:
time: 735 us; the launch traced here: 727 us
  waiting for transfers between devices  601 us (82%)
  blocking collectives  52.1 us (7%)
  matrix products  42.9 us (6%)
  between operations  13.7 us (2%)
  local copies, waits for them, and re-layouts  11.9 us (2%)
    reduce_scatter x1, waiting for transfers between devices, shards(): lax.psum_scatter(jnp.dot(one_hot(far_col, lax.axis_size(('sub', 'lvl')) *...  601 us
    all_gather x1, blocking collectives, shards(): lax.all_gather(root.reshape(1, 2 * rank), ('sub', 'lvl'), axis=0, tiled=T...  52.1 us
  transfers between devices with their start and end apart: 4, of which 1 were waited for; matrix products, arithmetic and copies ran while one was open for 7% of the time, Pallas kernels for 0%

commit v1 on v0

v1 whole, which is shorter than its diff:
```python
import jax
import jax.numpy as jnp
from jax import lax
from jax.experimental import pallas as pl
from jax.experimental.pallas import tpu as pltpu
from jax.sharding import PartitionSpec as P

F32 = jnp.float32
BF16 = jnp.bfloat16
MESH = pl.DeviceIdType.MESH
OFFSETS = (-3, -2, -1, 1, 2, 3)
LEVELS = ((0, 32), (32, 16), (48, 8), (56, 4), (60, 2))


def dot(a, b, ca, cb):
    return lax.dot_general(a, b, (((ca,), (cb,)), ((), ())), preferred_element_type=F32)


def nn(a, b):
    return dot(a, b, 1, 0)


def nt(a, b):
    return dot(a, b, 1, 1)


def tn(a, b):
    return dot(a, b, 0, 0)


def split(x):
    hi = x.astype(BF16)
    return hi, (x - hi.astype(F32)).astype(BF16)


def pick(one_hot, x):
    hi, lo = split(x)
    return nn(one_hot, hi) + nn(one_hot, lo)


def iota(shape, dim):
    return lax.broadcasted_iota(jnp.int32, shape, dim)


def doubled(flat):
    turned = pltpu.roll(flat, 64, 1)
    low = iota(flat.shape, 1) < 64
    return jnp.where(low, flat, turned), jnp.where(low, turned, flat)


def spread(rows, blocks):
    row = iota((16, 128), 0) % 8
    half = iota((16, 128), 1) // 64
    return jnp.concatenate(
        [jnp.where(row == 2 * t + half, rows, 0.0) for t in range(blocks // 2)], axis=1
    )


def collect(wide, blocks):
    row = iota((16, 128), 0) % 8
    half = iota((16, 128), 1) // 64
    total = jnp.zeros((16, 128), F32)
    for t in range(blocks // 2):
        total = total + jnp.where(row == 2 * t + half, wide[:, 128 * t : 128 * t + 128], 0.0)
    return total + pltpu.roll(total, 64, 1)


def joined(rows):
    return jnp.concatenate([rows[0:8, 0:64], rows[8:16, 0:64]], axis=1)


def tree_up(cs, ps, trans):
    for offset, width in LEVELS:
        count = min(width, 8)
        for g in range(width // count):
            d0, d1 = doubled(cs[8 * g : 8 * g + 8, :])
            lh, ll = split(spread(jnp.concatenate([d0, d1], axis=0), count))
            e = trans[offset + 8 * g : offset + 8 * g + count].reshape(64 * count, 64)
            eh, el = split(e)
            ps[8 * g : 8 * g + 8, :] = joined(nn(lh, eh) + nn(ll, eh) + nn(lh, el))
        half = width // 2
        cs[0:half, :] = ps[pl.ds(0, half, stride=2), :] + ps[pl.ds(1, half, stride=2), :]


def tree_down(fs, trans):
    for offset, width in reversed(LEVELS):
        count = min(width, 8)
        groups = []
        for g in range(width // count):
            f = jnp.concatenate([fs[0, 8 * g : 8 * g + 8, :], fs[1, 8 * g : 8 * g + 8, :]], axis=0)
            fh, fl = split(f[:, 0:64])
            e = trans[offset + 8 * g : offset + 8 * g + count].reshape(64 * count, 64)
            eh, el = split(e)
            groups.append(collect(nt(fh, eh) + nt(fl, eh) + nt(fh, el), count))
        for g, child in enumerate(groups):
            for v in range(2):
                if offset == 0:
                    fs[v, 8 * g : 8 * g + 8, :] = child[8 * v : 8 * v + 8]
                else:
                    fs[v, pl.ds(16 * g, 8, stride=2), :] = child[8 * v : 8 * v + 8]
                    fs[v, pl.ds(16 * g + 1, 8, stride=2), :] = child[8 * v : 8 * v + 8]


def kernel(
    vec, near_row, near_col, far_row, far_col,
    self_h, near_h, base_h, trans_h, coup_h, root_h,
    out,
    selfs, nears, bases, trans, coup, roots,
    x32, xs, xn, cs, ps, fs, coupb, bwd, fwd, leaf, nearp, nwork, back, backin,
    ga, gb, gc, gcin, nsend, nrecv,
    load_sem, a_send, a_recv, b_send, b_recv, c_send, c_recv, o_send, o_recv,
):
    s = lax.axis_index("sub")
    y = lax.axis_index("lvl")
    z = lax.div(s, 8)
    x = lax.rem(lax.div(s, 2), 4)
    c = lax.rem(s, 2)
    me = s * 4 + y

    loads = []
    for i, (src, dst) in enumerate(
        ((base_h, bases), (coup_h, coup), (trans_h, trans), (self_h, selfs), (near_h, nears), (root_h, roots))
    ):
        load = pltpu.make_async_copy(src, dst, load_sem.at[i])
        load.start()
        loads.append(load)

    def along(dim, o):
        if dim == "y":
            return s, lax.rem(y + o, 4)
        if dim == "x":
            return (z * 4 + lax.rem(x + o, 4)) * 2 + c, y
        return (lax.rem(z + o, 4) * 4 + x) * 2 + c, y

    sibling = ((z * 4 + x) * 2 + 1 - c, y)

    def shifted(o):
        m = lax.rem(me + o + 128, 128)
        return lax.div(m, 4), lax.rem(m, 4)

    barrier = pltpu.get_barrier_semaphore()
    peers = [along(d, o) for d in "xyz" for o in (1, 2, 3)] + [sibling] + [shifted(o) for o in OFFSETS]
    for peer in peers:
        pl.semaphore_signal(barrier, inc=1, device_id=peer, device_id_type=MESH)

    pending = []

    def send(src, dst, ssem, rsem, peer):
        copy = pltpu.make_async_remote_copy(
            src_ref=src, dst_ref=dst, send_sem=ssem, recv_sem=rsem, device_id=peer, device_id_type=MESH
        )
        copy.start()
        pending.append(copy)

    def arrive(dst, ssem, rsem):
        pltpu.make_async_remote_copy(
            src_ref=dst, dst_ref=dst, send_sem=ssem, recv_sem=rsem, device_id=sibling, device_id_type=MESH
        ).wait_recv()

    place = {"x": x, "y": y, "z": z}

    class Stream:
        def __init__(self, ref, order, ssem, rsem):
            self.ref, self.ssem, self.rsem = ref, ssem, rsem
            self.dims = order
            self.f, self.s, self.t = (place[d] for d in order)

        def chunk(self, phase, o):
            if phase == 0:
                return self.ref.at[c, self.t, self.s, lax.rem(self.f + 4 - o, 4)]
            if phase == 1:
                return self.ref.at[c, self.t, lax.rem(self.s + 4 - o, 4)]
            return self.ref.at[c, lax.rem(self.t + 4 - o, 4)]

        def push(self, phase):
            mine = self.chunk(phase, 0)
            for o in (1, 2, 3):
                k = 3 * phase + o - 1
                send(mine, mine, self.ssem.at[k], self.rsem.at[k], along(self.dims[phase], o))
            if phase == 2:
                self.over(0)

        def pull(self, phase, o):
            k = 3 * phase + o - 1
            arrive(self.chunk(phase, o), self.ssem.at[k], self.rsem.at[k])

        def over(self, o):
            mine = self.chunk(2, o)
            send(mine, mine, self.ssem.at[9 + o], self.rsem.at[9 + o], sibling)

        def pull_over(self, o):
            k = 9 + o
            dst = self.ref.at[1 - c, lax.rem(self.t + 4 - o, 4)]
            arrive(dst, self.ssem.at[k], self.rsem.at[k])

        def pull_all(self, phase):
            for o in (1, 2, 3):
                self.pull(phase, o)
                if phase == 2:
                    self.over(o)

    sa = Stream(ga, "zxy", a_send, a_recv)
    sb = Stream(gb, "yxz", b_send, b_recv)
    sc = Stream(gc, "yxz", c_send, c_recv)

    for v in range(2):
        xv = vec[:, v, :].astype(F32)
        x32[v, 0:32, :] = xv
        xs[v] = xv.astype(BF16)

    row16 = iota((16, 256), 0) % 8
    far_r = far_row[...]
    far_c = far_col[...]
    own_hot = (iota((32, 128), 0) == far_r).astype(BF16)

    loads[0].wait()

    def coeff_group(g, carry):
        xg = jnp.concatenate([x32[0, pl.ds(8 * g, 8), :], x32[1, pl.ds(8 * g, 8), :]], axis=0)
        lhs = jnp.concatenate([jnp.where(row16 == j, xg, 0.0).astype(BF16) for j in range(8)], axis=1)
        cs[pl.ds(8 * g, 8), :] = joined(nn(lhs, bases[pl.ds(8 * g, 8)].reshape(2048, 64)))
        return carry

    lax.fori_loop(0, 4, coeff_group, 0)
    cb = cs[...].astype(BF16)
    ga[c, y, x, z] = cb
    pl.semaphore_wait(barrier, len(peers))
    sa.push(0)
    send(xs, xn, o_send.at[0], o_recv.at[0], shifted(-1))

    ch, cl = split(cs[...])
    d0, d1 = doubled(tn(own_hot, ch) + tn(own_hot, cl))
    bwd[0] = d0
    bwd[1] = d1
    loads[1].wait()

    def back_group(g, carry):
        rows = jnp.concatenate([bwd[0, pl.ds(8 * g, 8), :], bwd[1, pl.ds(8 * g, 8), :]], axis=0)
        wh, wl = split(coup[pl.ds(8 * g, 8)].reshape(512, 64))
        coupb[0, pl.ds(8 * g, 8)] = wh.reshape(8, 64, 64)
        coupb[1, pl.ds(8 * g, 8)] = wl.reshape(8, 64, 64)
        lh, ll = split(spread(rows, 8))
        fwd[pl.ds(8 * g, 8), :] = joined(nn(lh, wh) + nn(ll, wh) + nn(lh, wl))
        return carry

    lax.fori_loop(0, 16, back_group, 0)
    bh, bl = split(fwd[...])
    dev = far_c // 32
    dist = (dev - me + 128) % 128
    is_far = (dist > 3) & (dist < 125)
    before = (iota((128, 128), 0) < iota((128, 128), 1)).astype(BF16)
    pos = nn(jnp.broadcast_to(is_far.astype(F32), (16, 128)).astype(BF16), before)[0:1, :].astype(jnp.int32)
    pos = jnp.where(is_far, pos, -1000)
    far_hot = (iota((32, 128), 0) == pos).astype(BF16)
    gb[c, z, x, y] = nn(far_hot, bh).astype(BF16)
    sb.push(0)
    leaf_of = iota((32, 128), 0)
    near_hot = jnp.concatenate(
        [(leaf_of + ((me + o + 128) % 128) * 32 == far_c).astype(BF16) for o in OFFSETS], axis=0
    )
    nsend[...] = (nn(near_hot, bh) + nn(near_hot, bl)).astype(BF16).reshape(6, 32, 128)
    for i, o in enumerate(OFFSETS):
        send(nsend.at[i], nrecv.at[i], o_send.at[2 + i], o_recv.at[2 + i], shifted(o))

    for o in (1, 2, 3):
        sa.pull(0, o)
    sa.push(1)

    loads[2].wait()
    tree_up(cs, ps, trans)
    rh, rl = split(cs[0:1, :])
    lane_hot = (iota((128, 128), 0) == pos + 32 * y).astype(BF16)
    row_id = iota((16, 128), 0)
    codes = jnp.where(row_id == 0, dev, jnp.where(row_id == 1, far_c - dev * 32, 0)).astype(F32).astype(BF16)
    tile = nt(codes, lane_hot)
    tile = jnp.where(row_id == 4 + 2 * y, rh.astype(F32), tile)
    tile = jnp.where(row_id == 5 + 2 * y, rl.astype(F32), tile)
    gcin[y] = tile.astype(BF16)
    for o in (1, 2, 3):
        send(gcin.at[y], gcin.at[y], c_send.at[o - 1], c_recv.at[o - 1], along("y", o))

    sa.pull_all(1)
    sa.push(2)
    sb.pull_all(0)
    sb.push(1)
    for o in (1, 2, 3):
        arrive(gcin.at[lax.rem(y + 4 - o, 4)], c_send.at[o - 1], c_recv.at[o - 1])
    merged = gcin[0].astype(F32) + gcin[1].astype(F32) + gcin[2].astype(F32) + gcin[3].astype(F32)
    gc[c, z, x] = merged.astype(BF16)
    for o in (1, 2, 3):
        send(gc.at[c, z, x], gc.at[c, z, x], c_send.at[2 + o], c_recv.at[2 + o], along("x", o))

    def group_rows(ref, g):
        return jnp.concatenate([ref[0, pl.ds(8 * g, 8), :], ref[1, pl.ds(8 * g, 8), :]], axis=0)

    def run_blocks(src, dst, blocks, product, add):
        def body(g, carry):
            rows = group_rows(src, g)
            acc = jnp.zeros((16, 256), F32)
            for j in range(8):
                acc = acc + product(jnp.where(row16 == j, rows, 0.0).astype(BF16), blocks[8 * g + j])
            for v in range(2):
                part = acc[8 * v : 8 * v + 8]
                if add:
                    part = part + dst[v, pl.ds(8 * g, 8), :]
                dst[v, pl.ds(8 * g, 8), :] = part
            return carry

        lax.fori_loop(0, 4, body, 0)

    loads[3].wait()
    run_blocks(x32, nearp, selfs, nt, False)

    sb.pull_all(1)
    sb.push(2)
    for o in (1, 2, 3):
        arrive(gc.at[c, z, lax.rem(x + 4 - o, 4)], c_send.at[2 + o], c_recv.at[2 + o])
    for o in (1, 2, 3):
        send(gc.at[c, z], gc.at[c, z], c_send.at[5 + o], c_recv.at[5 + o], along("z", o))
    sc.over(0)
    sa.pull_all(2)

    row_hot = (iota((32, 32), 0) == near_row[...]).astype(BF16)
    col_hot = (iota((64, 32), 0) == near_col[...]).astype(BF16)
    for v in range(2):
        nwork[v] = tn(row_hot, xs[v])
    loads[4].wait()
    run_blocks(nwork, nwork, nears, nn, False)
    for v in range(2):
        both = pick(col_hot, nwork[v])
        nearp[v] = nearp[v] + both[0:32]
        back[v] = both[32:64]
    send(back, backin, o_send.at[1], o_recv.at[1], shifted(1))

    sc.pull_all(2)
    sb.pull_all(2)

    arrive(xn, o_send.at[0], o_recv.at[0])
    for v in range(2):
        nwork[v] = tn(col_hot, jnp.concatenate([xs[v], xn[v]], axis=0))
    run_blocks(nwork, nwork, nears, nt, False)
    for v in range(2):
        nearp[v] = nearp[v] + pick(row_hot, nwork[v])

    for o in range(4):
        sc.pull_over(o)
    loads[5].wait()

    def root_group(i, carry):
        acc0, acc1 = carry
        t = gc[lax.rem(i, 2), lax.div(i, 8), lax.rem(lax.div(i, 2), 4)].astype(F32)
        turned = pltpu.roll(t, 64, 1)
        for k in range(4):
            m = roots[0, 4 * i + k]
            acc0 = acc0 + m * (t[4 + 2 * k : 5 + 2 * k, 0:64] + t[5 + 2 * k : 6 + 2 * k, 0:64])
            acc1 = acc1 + m * (turned[4 + 2 * k : 5 + 2 * k, 0:64] + turned[5 + 2 * k : 6 + 2 * k, 0:64])
        return acc0, acc1

    zero = jnp.zeros((64, 64), F32)
    tops = lax.fori_loop(0, 32, root_group, (zero, zero))
    ones = jnp.ones((16, 64), BF16)
    for v in range(2):
        th, tl = split(tops[v])
        top = (nt(ones, th) + nt(ones, tl))[0:8]
        fs[v, 0:8, :] = jnp.concatenate([top, top], axis=1)
    tree_down(fs, trans)

    for o in range(4):
        sa.pull_over(o)
    ldev = far_c // 32
    perm = ((ldev // 4) % 2) * 64 + (ldev % 4) * 16 + ((ldev // 8) % 4) * 4 + ldev // 32
    code = (perm * 32 + far_c - ldev * 32).astype(F32)
    codes_q = jnp.transpose(jnp.broadcast_to(code, (128, 128)))
    lane = iota((128, 128), 1).astype(F32)
    partner = jnp.zeros((128, 128), F32)
    for i in range(8):
        for j in range(4):
            base = float(128 * (i * 4 + j))
            hot = (codes_q == lane + base).astype(BF16)
            partner = partner + nn(hot, ga[i // 4, i % 4, j].reshape(128, 128))
    bwd[0] = partner
    bwd[1] = pltpu.roll(partner, 64, 1)

    def fwd_group(g, carry):
        rows = group_rows(bwd, g)[:, 0:64].astype(BF16)
        wide = nt(rows, coupb[0, pl.ds(8 * g, 8)].reshape(512, 64))
        wide = wide + nt(rows, coupb[1, pl.ds(8 * g, 8)].reshape(512, 64))
        r = collect(wide, 8)
        fwd[pl.ds(8 * g, 8), :] = jnp.where(iota((8, 128), 1) < 64, r[0:8], r[8:16])
        return carry

    lax.fori_loop(0, 16, fwd_group, 0)
    acc = pick(own_hot, fwd[...])

    for o in range(4):
        sb.pull_over(o)

    for i in range(2):
        for j in range(4):
            for k in range(4):
                t = gc[i, j, k].astype(F32)
                hot = ((t[0:1, :] == me.astype(F32)) & (t[1:2, :] == leaf_of.astype(F32))).astype(BF16)
                acc = acc + nn(hot, gb[i, j, k].reshape(128, 128))
    for i in range(6):
        arrive(nrecv.at[i], o_send.at[2 + i], o_recv.at[2 + i])
        acc = acc + nrecv[i].astype(F32)

    field = acc + jnp.where(iota((32, 128), 1) < 64, fs[0], fs[1])
    d0, d1 = doubled(field.astype(BF16).astype(F32))
    fs[0] = d0
    fs[1] = d1
    arrive(backin, o_send.at[1], o_recv.at[1])

    def out_group(g, carry):
        rows = group_rows(fs, g)[:, 0:64]
        acc = jnp.zeros((16, 256), F32)
        mask = iota((16, 64), 0) % 8
        for j in range(8):
            acc = acc + nt(jnp.where(mask == j, rows, 0.0).astype(BF16), bases[8 * g + j])
        for v in range(2):
            here = pl.ds(8 * g, 8)
            out[v, here, :] = acc[8 * v : 8 * v + 8] + nearp[v, here, :] + backin[v, here, :]
        return carry

    lax.fori_loop(0, 4, out_group, 0)
    for copy in pending:
        copy.wait_send()


def shards(
    vectors, self_blocks, near_blocks, near_row, near_col, bases, transfers, far_row, far_col, couplings,
    root_couplings,
):
    vmem = pl.BlockSpec(memory_space=pltpu.VMEM)
    hbm = pl.BlockSpec(memory_space=pl.ANY)
    result = pl.pallas_call(
        kernel,
        out_shape=jax.ShapeDtypeStruct((2, 32, 256), F32),
        in_specs=[vmem] * 5 + [hbm] * 6,
        out_specs=vmem,
        scratch_shapes=[
            pltpu.VMEM((32, 256, 256), BF16),
            pltpu.VMEM((32, 256, 256), BF16),
            pltpu.VMEM((32, 256, 64), BF16),
            pltpu.VMEM((62, 64, 64), F32),
            pltpu.VMEM((128, 64, 64), F32),
            pltpu.VMEM((1, 128, 64, 64), F32),
            pltpu.VMEM((2, 32, 256), F32),
            pltpu.VMEM((2, 32, 256), BF16),
            pltpu.VMEM((2, 32, 256), BF16),
            pltpu.VMEM((32, 128), F32),
            pltpu.VMEM((32, 128), F32),
            pltpu.VMEM((2, 32, 128), F32),
            pltpu.VMEM((2, 128, 64, 64), BF16),
            pltpu.VMEM((2, 128, 128), F32),
            pltpu.VMEM((128, 128), F32),
            pltpu.VMEM((32, 128), F32),
            pltpu.VMEM((2, 32, 256), F32),
            pltpu.VMEM((2, 32, 256), F32),
            pltpu.VMEM((2, 32, 256), F32),
            pltpu.VMEM((2, 32, 256), F32),
            pltpu.VMEM((2, 4, 4, 4, 32, 128), BF16),
            pltpu.VMEM((2, 4, 4, 4, 32, 128), BF16),
            pltpu.VMEM((2, 4, 4, 16, 128), BF16),
            pltpu.VMEM((4, 16, 128), BF16),
            pltpu.VMEM((6, 32, 128), BF16),
            pltpu.VMEM((6, 32, 128), BF16),
            pltpu.SemaphoreType.DMA((6,)),
            pltpu.SemaphoreType.DMA((13,)),
            pltpu.SemaphoreType.DMA((13,)),
            pltpu.SemaphoreType.DMA((13,)),
            pltpu.SemaphoreType.DMA((13,)),
            pltpu.SemaphoreType.DMA((13,)),
            pltpu.SemaphoreType.DMA((13,)),
            pltpu.SemaphoreType.DMA((8,)),
            pltpu.SemaphoreType.DMA((8,)),
        ],
        compiler_params=pltpu.CompilerParams(
            collective_id=0, has_side_effects=True, vmem_limit_bytes=50 * 1024 * 1024
        ),
    )(
        vectors, near_row.reshape(1, 32), near_col.reshape(1, 32), far_row.reshape(1, 128), far_col.reshape(1, 128),
        self_blocks, near_blocks, bases, transfers, couplings, root_couplings,
    )
    return result.transpose(1, 0, 2)


def solution(mesh):
    both = ("sub", "lvl")
    in_specs = (
        P(both, None, None), P(both, None, None), P(both, None, None), P(both), P(both), P(both, None, None),
        P(both, None, None), P(both), P(both), P(both, None, None), P(both, None, None, None),
    )
    return jax.shard_map(shards, mesh=mesh, in_specs=in_specs, out_specs=P(both, None, None), check_vma=False)
```

time: 735 us -> 56.1 us (0.08); the launches traced: 727 us -> 56.1 us
  waiting for transfers between devices: 601 us -> 0 us
  blocking collectives: 52.1 us -> 0 us
  matrix products: 42.9 us -> 0 us
  Pallas kernels: 0 us -> 42.2 us
  between operations: 13.7 us -> 0.06 us
    reduce_scatter x1 -> x0, waiting for transfers between devices: 601 us -> none  [shards(): lax.psum_scatter(jnp.dot(one_hot(far_col, lax.axis_size(('sub', 'lvl')) *...]
    all_gather x1 -> x0, blocking collectives: 52.1 us -> none  [shards(): lax.all_gather(root.reshape(1, 2 * rank), ('sub', 'lvl'), axis=0, tiled=T...]
    dot_general x22 -> x0, matrix products: 42.9 us -> none  [the longest x5 8.7 us: tree_down(): jnp.einsum('nkr,nvr->nvk', trans[offset:offset + width], jnp.repeat(field...]
    pallas_call x0 -> x1, Pallas kernels: none -> 42.2 us  [shards(): pl.pallas_call(kernel, out_shape=jax.ShapeDtypeStruct((2, 32, 256), F32),...]
    unnamed x19 -> x17, local copies, waits for them, and re-layouts: 5.75 us -> 13.1 us
  transfers between devices with their start and end apart: 4 -> 0, of which waited for: 1 -> 0; matrix products, arithmetic and copies ran while one was open for 7% -> 0% of each run, Pallas kernels for 0% -> 0%
where the time goes in v1:
time: 56.1 us
  Pallas kernels  42.2 us (75%)
  local copies, waits for them, and re-layouts  13.8 us (25%)
    pallas_call x1, Pallas kernels, shards(): pl.pallas_call(kernel, out_shape=jax.ShapeDtypeStruct((2, 32, 256), F32),...  42.2 us
    unnamed x17, local copies, waits for them, and re-layouts  13.1 us

profile of v1, /device:TPU:1, one launch (start us, length us, event | category | flops | bytes accessed | tf_op | source)
XLA Modules:
  0.0 56.1 jit_solution(15158801785916859166)
XLA Ops:
  0.0 0.0 copy-start.6
  0.0 2.9 %copy.12.base_h = bf16[32,256,64]{2,1,0:T(8,128)(2,1)} copy(bf16[32,256,64]{1,2,0:T(8,128)(2,1)} %param.16) | data formatting | bytes 2097152 | tf_op args[5]
  2.9 0.0 copy-done.6
  2.9 4.5 %copy.13.coup_h = f32[128,64,64]{2,1,0:T(8,128)} copy(f32[128,64,64]{0,2,1:T(8,128)S(1)} %copy-done.6) | data formatting | bytes 4194304 | tf_op args[9]
  7.4 0.0 copy-start
  7.4 0.0 copy-start.1
  7.4 0.0 copy-start.2
  7.4 0.0 copy-start.3
  7.4 0.0 copy-start.4
  7.4 0.0 copy-start.5
  7.4 5.7 %copy.14.root_h = f32[1,128,64,64]{3,2,1,0:T(8,128)} copy(f32[1,128,64,64]{1,3,2,0:T(8,128)} %param.21) | data formatting | bytes 4194304 | tf_op args[10]
  13.1 0.0 copy-done
  13.2 0.0 copy-done.1
  13.2 0.0 copy-done.2
  13.2 0.0 copy-done.3
  13.2 0.0 copy-done.4
  13.2 0.0 copy-done.5
  13.2 42.2 %shard_map.109 = f32[2,32,256]{2,1,0:T(8,128)S(1)} custom-call(bf16[32,2,256]{2,1,0:T(2,128)(2,1)S(1)} %copy-done.1, s32[1,32]{1,0:T(1,128)S(1)} %bitcast.6, s32[1,32]{1,0:T(1,128)S(1)} %bitcast.7, s32[1,128]{1,0:T(1,128)S(1)} %bitcast.8, s32[1,128]{1,0:T(1,128)S(1)} %bitcast.9, bf16[32,256,256]{2,1,0:T(8,128)(2,1)} %self_h.1, bf16[32,256,256]{2,1,0:T(8,128)(2,1)} %near_h.1, ...), custom_call_target="tpu_custom_call" | custom-call | tf_op jit(solution)/shard_map/pallas_call | solution.py:436
  55.4 0.7 %copy.15 = f32[32,2,256]{2,1,0:T(2,128)} copy(f32[32,2,256]{2,0,1:T(8,128)S(1)} %bitcast.5) | data formatting | bytes 131072 | tf_op jit(solution)/shard_map/transpose | solution.py:485
Async XLA Ops:
  0.0 2.9 %copy-start.6 = (f32[128,64,64]{0,2,1:T(8,128)S(1)}, f32[128,64,64]{0,2,1:T(8,128)}, u32[]{:S(2)}) copy-start(f32[128,64,64]{0,2,1:T(8,128)} %param.20) | copy-start | bytes 6291460
  7.4 5.8 %copy-start = (f32[62,64,64]{2,1,0:T(8,128)S(1)}, f32[62,64,64]{2,1,0:T(8,128)}, u32[]{:S(2)}) copy-start(f32[62,64,64]{2,1,0:T(8,128)} %trans_h.1) | copy-start | bytes 3047428
  7.4 5.8 %copy-start.1 = (bf16[32,2,256]{2,1,0:T(2,128)(2,1)S(1)}, bf16[32,2,256]{2,1,0:T(2,128)(2,1)}, u32[]{:S(2)}) copy-start(bf16[32,2,256]{2,1,0:T(2,128)(2,1)} %vec.1) | copy-start | bytes 98308
  7.4 5.8 %copy-start.2 = (s32[32]{0:T(128)S(1)}, s32[32]{0:T(128)}, u32[]{:S(2)}) copy-start(s32[32]{0:T(128)} %param.14) | copy-start | bytes 388
  7.4 5.8 %copy-start.3 = (s32[32]{0:T(128)S(1)}, s32[32]{0:T(128)}, u32[]{:S(2)}) copy-start(s32[32]{0:T(128)} %param.15) | copy-start | bytes 388
  7.4 5.8 %copy-start.4 = (s32[128]{0:T(128)S(1)}, s32[128]{0:T(128)}, u32[]{:S(2)}) copy-start(s32[128]{0:T(128)} %param.18) | copy-start | bytes 1540
  7.4 5.8 %copy-start.5 = (s32[128]{0:T(128)S(1)}, s32[128]{0:T(128)}, u32[]{:S(2)}) copy-start(s32[128]{0:T(128)} %param.19) | copy-start | bytes 1540

commit v2 on v1

v2 whole, which is shorter than its diff:
```python
import jax
import jax.numpy as jnp
from jax import lax
from jax.experimental import pallas as pl
from jax.experimental.pallas import tpu as pltpu
from jax.sharding import PartitionSpec as P

F32 = jnp.float32
BF16 = jnp.bfloat16
MESH = pl.DeviceIdType.MESH
OFFSETS = (-3, -2, -1, 1, 2, 3)
LEVELS = ((0, 32), (32, 16), (48, 8), (56, 4), (60, 2))


def dot(a, b, ca, cb):
    return lax.dot_general(a, b, (((ca,), (cb,)), ((), ())), preferred_element_type=F32)


def nn(a, b):
    return dot(a, b, 1, 0)


def nt(a, b):
    return dot(a, b, 1, 1)


def tn(a, b):
    return dot(a, b, 0, 0)


def split(x):
    hi = x.astype(BF16)
    return hi, (x - hi.astype(F32)).astype(BF16)


def pick(one_hot, x):
    hi, lo = split(x)
    return nn(one_hot, hi) + nn(one_hot, lo)


def iota(shape, dim):
    return lax.broadcasted_iota(jnp.int32, shape, dim)


def doubled(flat):
    turned = pltpu.roll(flat, 64, 1)
    low = iota(flat.shape, 1) < 64
    return jnp.where(low, flat, turned), jnp.where(low, turned, flat)


def spread(rows, blocks):
    row = iota((16, 128), 0) % 8
    half = iota((16, 128), 1) // 64
    return jnp.concatenate(
        [jnp.where(row == 2 * t + half, rows, 0.0) for t in range(blocks // 2)], axis=1
    )


def collect(wide, blocks):
    row = iota((16, 128), 0) % 8
    half = iota((16, 128), 1) // 64
    total = jnp.zeros((16, 128), F32)
    for t in range(blocks // 2):
        total = total + jnp.where(row == 2 * t + half, wide[:, 128 * t : 128 * t + 128], 0.0)
    return total + pltpu.roll(total, 64, 1)


def joined(rows):
    return jnp.concatenate([rows[0:8, 0:64], rows[8:16, 0:64]], axis=1)


def abreast(rows):
    return jnp.where(iota((8, 128), 1) < 64, rows[0:8], rows[8:16])


def contract(mats, terms, dst):
    t = terms[...]

    def body(i, carry):
        for j in range(8):
            m = mats[8 * i + j]
            for v in range(2):
                row = jnp.sum(m * t[64 * v : 64 * v + 64], axis=0, keepdims=True)
                dst[pl.ds(64 * v + 8 * i + j, 1), :] = row
        return carry

    lax.fori_loop(0, 8, body, 0)


def contract_turned(mats, terms, dst):
    def body(i, carry):
        acc0, acc1 = carry
        for j in range(8):
            m = mats[8 * i + j]
            acc0 = acc0 + m * terms[pl.ds(8 * i + j, 1), :]
            acc1 = acc1 + m * terms[pl.ds(64 + 8 * i + j, 1), :]
        return acc0, acc1

    zero = jnp.zeros((64, 128), F32)
    acc0, acc1 = lax.fori_loop(0, 8, body, (zero, zero))
    dst[0:64, :] = acc0
    dst[64:128, :] = acc1


def tree_up(cs, ps, trans):
    for offset, width in LEVELS:
        count = min(width, 8)
        for g in range(width // count):
            d0, d1 = doubled(cs[8 * g : 8 * g + 8, :])
            lh, ll = split(spread(jnp.concatenate([d0, d1], axis=0), count))
            e = trans[offset + 8 * g : offset + 8 * g + count].reshape(64 * count, 64)
            eh, el = split(e)
            ps[8 * g : 8 * g + 8, :] = joined(nn(lh, eh) + nn(ll, eh) + nn(lh, el))
        half = width // 2
        cs[0:half, :] = ps[pl.ds(0, half, stride=2), :] + ps[pl.ds(1, half, stride=2), :]


def tree_down(fs, trans):
    for offset, width in reversed(LEVELS):
        count = min(width, 8)
        groups = []
        for g in range(width // count):
            f = jnp.concatenate([fs[0, 8 * g : 8 * g + 8, :], fs[1, 8 * g : 8 * g + 8, :]], axis=0)
            fh, fl = split(f[:, 0:64])
            e = trans[offset + 8 * g : offset + 8 * g + count].reshape(64 * count, 64)
            eh, el = split(e)
            groups.append(collect(nt(fh, eh) + nt(fl, eh) + nt(fh, el), count))
        for g, child in enumerate(groups):
            for v in range(2):
                if offset == 0:
                    fs[v, 8 * g : 8 * g + 8, :] = child[8 * v : 8 * v + 8]
                else:
                    fs[v, pl.ds(16 * g, 8, stride=2), :] = child[8 * v : 8 * v + 8]
                    fs[v, pl.ds(16 * g + 1, 8, stride=2), :] = child[8 * v : 8 * v + 8]


def kernel(
    vec_h, near_row_h, near_col_h, far_row_h, far_col_h,
    self_h, near_h, base_h, trans_h, coup_h, root_h,
    out,
    vec, near_row, near_col, far_row, far_col,
    selfs, nears, bases, trans, coup, roots,
    x32, xs, xn, cs, ps, fs, terms, sums, nearp, nwork, back, backin,
    ga, gb, gc, gcin, nsend, nrecv,
    load_sem, send_sem, a_recv, b_recv, c_recv, o_recv,
):
    s = lax.axis_index("sub")
    y = lax.axis_index("lvl")
    z = lax.div(s, 8)
    x = lax.rem(lax.div(s, 2), 4)
    c = lax.rem(s, 2)
    me = s * 4 + y

    loads = []
    for i, (src, dst) in enumerate(
        (
            (vec_h, vec), (far_row_h, far_row), (far_col_h, far_col), (near_row_h, near_row), (near_col_h, near_col),
            (base_h, bases), (coup_h, coup), (trans_h, trans), (self_h, selfs), (near_h, nears), (root_h, roots),
        )
    ):
        load = pltpu.make_async_copy(src, dst, load_sem.at[i])
        load.start()
        loads.append(load)

    def at(x=0, y=0, z=0):
        ox, oy, oz = x, y, z
        return (
            (lax.rem(place["z"] + oz, 4) * 4 + lax.rem(place["x"] + ox, 4)) * 2 + c,
            lax.rem(place["y"] + oy, 4),
        )

    place = {"x": x, "y": y, "z": z}
    sibling = ((z * 4 + x) * 2 + 1 - c, y)

    def shifted(o):
        m = lax.rem(me + o + 128, 128)
        return lax.div(m, 4), lax.rem(m, 4)

    barrier = pltpu.get_barrier_semaphore()
    peers = [
        at(i, j, k)
        for i in range(4)
        for j in range(4)
        for k in range(4)
        if 0 < (i > 0) + (j > 0) + (k > 0) < 3
    ]
    peers = peers + [sibling] + [shifted(o) for o in OFFSETS]
    for peer in peers:
        pl.semaphore_signal(barrier, inc=1, device_id=peer, device_id_type=MESH)

    pending = []

    def send(src, dst, rsem, peer):
        copy = pltpu.make_async_remote_copy(
            src_ref=src, dst_ref=dst, send_sem=send_sem.at[len(pending)], recv_sem=rsem,
            device_id=peer, device_id_type=MESH,
        )
        copy.start()
        pending.append(copy)

    def arrive(dst, rsem):
        pltpu.make_async_remote_copy(
            src_ref=dst, dst_ref=dst, send_sem=send_sem.at[0], recv_sem=rsem,
            device_id=sibling, device_id_type=MESH,
        ).wait_recv()

    class Stream:
        def __init__(self, ref, order, rsem):
            self.ref, self.rsem, self.dims = ref, rsem, order
            self.f, self.s, self.t = (place[d] for d in order)

        def behind(self, index, o):
            return lax.rem(index + 4 - o, 4)

        def spread(self):
            mine = self.ref.at[c, self.t, self.s, self.f]
            for i in (2, 1, 3, 0):
                for j in (2, 1, 3, 0):
                    if i or j:
                        k = 4 * i + (j if i == 0 else 0)
                        send(mine, mine, self.rsem.at[k], at(**{self.dims[1]: i, self.dims[0]: j}))

        def relay(self, i):
            if i == 0:
                for j in (1, 2, 3):
                    arrive(self.ref.at[c, self.t, self.s, self.behind(self.f, j)], self.rsem.at[j])
            else:
                arrive(self.ref.at[c, self.t, self.behind(self.s, i)], self.rsem.at[4 * i])
            row = self.ref.at[c, self.t, self.behind(self.s, i)]
            for o in (2, 1, 3):
                send(row, row, self.rsem.at[16 + 4 * o + i], at(**{self.dims[2]: o}))

        def take(self, o):
            if o:
                for i in range(4):
                    arrive(self.ref.at[c, self.behind(self.t, o), self.behind(self.s, i)], self.rsem.at[16 + 4 * o + i])
            plane = self.ref.at[c, self.behind(self.t, o)]
            send(plane, plane, self.rsem.at[32 + o], sibling)
            return c, self.behind(self.t, o)

        def take_other(self, o):
            arrive(self.ref.at[1 - c, self.behind(self.t, o)], self.rsem.at[32 + o])
            return 1 - c, self.behind(self.t, o)

    sa = Stream(ga, "yxz", a_recv)
    sb = Stream(gb, "yzx", b_recv)

    for i in range(5):
        loads[i].wait()
    for v in range(2):
        xv = vec[:, v, :].astype(F32)
        x32[v, 0:32, :] = xv
        xs[v] = xv.astype(BF16)

    row16 = iota((16, 256), 0) % 8
    far_r = far_row[...]
    far_c = far_col[...]
    own_hot = (iota((32, 128), 0) == far_r).astype(BF16)

    def group_rows(ref, g):
        return jnp.concatenate([ref[0, pl.ds(8 * g, 8), :], ref[1, pl.ds(8 * g, 8), :]], axis=0)

    loads[5].wait()

    def coeff_group(g, carry):
        wide = nt(group_rows(x32, g).astype(BF16), bases[pl.ds(8 * g, 8)].reshape(512, 256))
        cs[pl.ds(8 * g, 8), :] = abreast(collect(wide, 8))
        return carry

    lax.fori_loop(0, 4, coeff_group, 0)
    ch, cl = split(cs[...])
    ga[c, z, x, y] = ch

    terms[...] = tn(ch, own_hot) + tn(cl, own_hot)
    loads[6].wait()
    contract_turned(coup, terms, sums)
    bh, bl = split(sums[...])
    dev = far_c // 32
    dist = (dev - me + 128) % 128
    is_far = (dist > 3) & (dist < 125)
    before = (iota((128, 128), 0) < iota((128, 128), 1)).astype(BF16)
    pos = nn(jnp.broadcast_to(is_far.astype(F32), (16, 128)).astype(BF16), before)[0:1, :].astype(jnp.int32)
    pos = jnp.where(is_far, pos, -1000)
    far_hot = (iota((32, 128), 0) == pos).astype(BF16)
    gb[c, x, z, y] = nt(far_hot, bh).astype(BF16)
    leaf_of = iota((32, 128), 0)
    near_hot = jnp.concatenate(
        [(leaf_of + ((me + o + 128) % 128) * 32 == far_c).astype(BF16) for o in OFFSETS], axis=0
    )
    nsend[...] = (nt(near_hot, bh) + nt(near_hot, bl)).astype(BF16).reshape(6, 32, 128)

    loads[7].wait()
    tree_up(cs, ps, trans)
    rh, rl = split(cs[0:1, :])
    lane_hot = (iota((128, 128), 0) == pos + 32 * y).astype(BF16)
    row_id = iota((16, 128), 0)
    codes = jnp.where(row_id == 0, dev, jnp.where(row_id == 1, far_c - dev * 32, 0)).astype(F32).astype(BF16)
    tile = nt(codes, lane_hot)
    tile = jnp.where(row_id == 4 + 2 * y, rh.astype(F32), tile)
    tile = jnp.where(row_id == 5 + 2 * y, rl.astype(F32), tile)
    gcin[y] = tile.astype(BF16)

    pl.semaphore_wait(barrier, len(peers))
    sa.spread()
    sb.spread()
    for o in (1, 2, 3):
        send(gcin.at[y], gcin.at[y], c_recv.at[o], at(y=o))
    send(xs, xn, o_recv.at[0], shifted(-1))
    for i, o in enumerate(OFFSETS):
        send(nsend.at[i], nrecv.at[i], o_recv.at[2 + i], shifted(o))

    def run_blocks(src, dst, blocks, product):
        def body(g, carry):
            rows = group_rows(src, g)
            acc = jnp.zeros((16, 256), F32)
            for j in range(8):
                acc = acc + product(jnp.where(row16 == j, rows, 0.0).astype(BF16), blocks[8 * g + j])
            for v in range(2):
                dst[v, pl.ds(8 * g, 8), :] = acc[8 * v : 8 * v + 8]
            return carry

        lax.fori_loop(0, 4, body, 0)

    loads[8].wait()
    run_blocks(x32, nearp, selfs, nt)

    row_hot = (iota((32, 32), 0) == near_row[...]).astype(BF16)
    col_hot = (iota((64, 32), 0) == near_col[...]).astype(BF16)
    for v in range(2):
        nwork[v] = tn(row_hot, xs[v])
    loads[9].wait()
    run_blocks(nwork, nwork, nears, nn)
    for v in range(2):
        both = pick(col_hot, nwork[v])
        nearp[v] = nearp[v] + both[0:32]
        back[v] = both[32:64]
    send(back, backin, o_recv.at[1], shifted(1))

    sa.relay(0)
    sb.relay(0)
    for o in (1, 2, 3):
        arrive(gcin.at[lax.rem(y + 4 - o, 4)], c_recv.at[o])
    merged = gcin[0].astype(F32) + gcin[1].astype(F32) + gcin[2].astype(F32) + gcin[3].astype(F32)
    gc[c, z, x] = merged.astype(BF16)
    for i in (2, 1, 3, 0):
        for j in (2, 1, 3, 0):
            if i or j:
                k = 4 + 4 * i + (j if i == 0 else 0)
                send(gc.at[c, z, x], gc.at[c, z, x], c_recv.at[k], at(z=i, x=j))
    for i in (1, 3, 2):
        sa.relay(i)
        sb.relay(i)

    arrive(xn, o_recv.at[0])
    for v in range(2):
        nwork[v] = tn(col_hot, jnp.concatenate([xs[v], xn[v]], axis=0))
    run_blocks(nwork, nwork, nears, nt)
    for v in range(2):
        nearp[v] = nearp[v] + pick(row_hot, nwork[v])

    ldev = far_c // 32
    perm = ((ldev // 4) % 2) * 64 + (ldev // 32) * 16 + ((ldev // 8) % 4) * 4 + ldev % 4
    code = (perm * 32 + far_c - ldev * 32).astype(F32)
    codes_q = jnp.transpose(jnp.broadcast_to(code, (128, 128)))
    lane = iota((128, 128), 1).astype(F32)

    def gather(place_a, partner):
        i, j = place_a
        for k in range(4):
            base = (((i * 4 + j) * 4 + k) * 128).astype(F32)
            partner = partner + nn((codes_q == lane + base).astype(BF16), ga[i, j, k].reshape(128, 128))
        return partner

    sa.take(0)
    sb.take(0)
    for i in range(4):
        if i:
            arrive(gc.at[c, lax.rem(z + 4 - i, 4)], c_recv.at[4 + 4 * i])
        else:
            for j in (1, 2, 3):
                arrive(gc.at[c, z, lax.rem(x + 4 - j, 4)], c_recv.at[4 + j])
    send(gc.at[c], gc.at[c], c_recv.at[0], sibling)
    partner = gather((c, z), jnp.zeros((128, 128), F32))
    for o in (1, 3, 2):
        where = sa.take(o)
        sb.take(o)
        partner = gather(where, partner)

    arrive(gc.at[1 - c], c_recv.at[0])
    row_at = iota((128, 512), 1)
    tile_at = row_at // 16
    line = row_at % 16
    holder = (((tile_at // 4) % 4 * 4 + tile_at % 4) * 2 + tile_at // 16) * 4 + (line - 4) // 2
    sel = ((holder == iota((128, 512), 0)) & (line >= 4) & (line < 12)).astype(BF16)
    terms[...] = jnp.transpose(nn(sel, gc[...].reshape(512, 128)))
    loads[10].wait()
    contract(roots, terms, sums)
    sh, sl = split(sums[...])
    ones = jnp.ones((16, 128), BF16)
    top = (nt(ones, sh) + nt(ones, sl))[0:8]
    d0, d1 = doubled(top)
    fs[0, 0:8, :] = d0
    fs[1, 0:8, :] = d1
    tree_down(fs, trans)

    for o in (0, 1, 3, 2):
        partner = gather(sa.take_other(o), partner)
    terms[...] = jnp.transpose(partner)
    contract(coup, terms, sums)
    sh, sl = split(sums[...])
    acc = nt(own_hot, sh) + nt(own_hot, sl)

    def deliver(place_b, acc):
        i, j = place_b
        for k in range(4):
            t = gc[i, k, j].astype(F32)
            hot = ((t[0:1, :] == me.astype(F32)) & (t[1:2, :] == leaf_of.astype(F32))).astype(BF16)
            acc = acc + nn(hot, gb[i, j, k].reshape(128, 128))
        return acc

    for o in range(4):
        acc = deliver((c, lax.rem(x + 4 - o, 4)), acc)
    for i in range(6):
        arrive(nrecv.at[i], o_recv.at[2 + i])
        acc = acc + nrecv[i].astype(F32)
    for o in (0, 1, 3, 2):
        acc = deliver(sb.take_other(o), acc)

    field = acc + jnp.where(iota((32, 128), 1) < 64, fs[0], fs[1])
    d0, d1 = doubled(field.astype(BF16).astype(F32))
    fs[0] = d0
    fs[1] = d1
    arrive(backin, o_recv.at[1])

    def out_group(g, carry):
        lhs = spread(group_rows(fs, g), 8).astype(BF16)
        acc = nn(lhs, bases[pl.ds(8 * g, 8)].reshape(512, 256))
        for v in range(2):
            here = pl.ds(8 * g, 8)
            out[v, here, :] = acc[8 * v : 8 * v + 8] + nearp[v, here, :] + backin[v, here, :]
        return carry

    lax.fori_loop(0, 4, out_group, 0)
    for copy in pending:
        copy.wait_send()


def shards(
    vectors, self_blocks, near_blocks, near_row, near_col, bases, transfers, far_row, far_col, couplings,
    root_couplings,
):
    vmem = pl.BlockSpec(memory_space=pltpu.VMEM)
    hbm = pl.BlockSpec(memory_space=pl.ANY)
    result = pl.pallas_call(
        kernel,
        out_shape=jax.ShapeDtypeStruct((2, 32, 256), F32),
        in_specs=[hbm] * 11,
        out_specs=vmem,
        scratch_shapes=[
            pltpu.VMEM((32, 2, 256), BF16),
            pltpu.VMEM((1, 32), jnp.int32),
            pltpu.VMEM((1, 32), jnp.int32),
            pltpu.VMEM((1, 128), jnp.int32),
            pltpu.VMEM((1, 128), jnp.int32),
            pltpu.VMEM((32, 256, 256), BF16),
            pltpu.VMEM((32, 256, 256), BF16),
            pltpu.VMEM((32, 64, 256), BF16),
            pltpu.VMEM((62, 64, 64), F32),
            pltpu.VMEM((64, 64, 128), F32),
            pltpu.VMEM((64, 64, 128), F32),
            pltpu.VMEM((2, 32, 256), F32),
            pltpu.VMEM((2, 32, 256), BF16),
            pltpu.VMEM((2, 32, 256), BF16),
            pltpu.VMEM((32, 128), F32),
            pltpu.VMEM((32, 128), F32),
            pltpu.VMEM((2, 32, 128), F32),
            pltpu.VMEM((128, 128), F32),
            pltpu.VMEM((128, 128), F32),
            pltpu.VMEM((2, 32, 256), F32),
            pltpu.VMEM((2, 32, 256), F32),
            pltpu.VMEM((2, 32, 256), F32),
            pltpu.VMEM((2, 32, 256), F32),
            pltpu.VMEM((2, 4, 4, 4, 32, 128), BF16),
            pltpu.VMEM((2, 4, 4, 4, 32, 128), BF16),
            pltpu.VMEM((2, 4, 4, 16, 128), BF16),
            pltpu.VMEM((4, 16, 128), BF16),
            pltpu.VMEM((6, 32, 128), BF16),
            pltpu.VMEM((6, 32, 128), BF16),
            pltpu.SemaphoreType.DMA((11,)),
            pltpu.SemaphoreType.DMA((104,)),
            pltpu.SemaphoreType.DMA((36,)),
            pltpu.SemaphoreType.DMA((36,)),
            pltpu.SemaphoreType.DMA((20,)),
            pltpu.SemaphoreType.DMA((8,)),
        ],
        compiler_params=pltpu.CompilerParams(
            collective_id=0, has_side_effects=True, vmem_limit_bytes=62 * 1024 * 1024
        ),
    )(
        vectors, near_row.reshape(1, 32), near_col.reshape(1, 32), far_row.reshape(1, 128), far_col.reshape(1, 128),
        self_blocks, near_blocks, bases.transpose(0, 2, 1), transfers, couplings.transpose(1, 2, 0),
        root_couplings[0].transpose(1, 2, 0),
    )
    return result.transpose(1, 0, 2)


def solution(mesh):
    both = ("sub", "lvl")
    in_specs = (
        P(both, None, None), P(both, None, None), P(both, None, None), P(both), P(both), P(both, None, None),
        P(both, None, None), P(both), P(both), P(both, None, None), P(both, None, None, None),
    )
    return jax.shard_map(shards, mesh=mesh, in_specs=in_specs, out_specs=P(both, None, None), check_vma=False)
```

time: 56.1 us -> 34.2 us (0.61)
  local copies, waits for them, and re-layouts: 13.8 us -> 1.52 us
  Pallas kernels: 42.2 us -> 32.5 us
    unnamed x17 -> x0, local copies, waits for them, and re-layouts: 13.1 us -> none
    pallas_call x1, Pallas kernels: 42.2 us -> 32.5 us  [shards(): pl.pallas_call(kernel, out_shape=jax.ShapeDtypeStruct((2, 32, 256), F32),...]
    transpose x1, local copies, waits for them, and re-layouts: 0.68 us -> 1.52 us  [shards(): return result.transpose(1, 0, 2)]
where the time goes in v2:
time: 34.2 us; the launch traced here: 34 us
  Pallas kernels  32.5 us (95%)
  local copies, waits for them, and re-layouts  1.52 us (4%)
    pallas_call x1, Pallas kernels, shards(): pl.pallas_call(kernel, out_shape=jax.ShapeDtypeStruct((2, 32, 256), F32),...  32.5 us
    transpose x1, local copies, waits for them, and re-layouts, shards(): return result.transpose(1, 0, 2)  1.52 us

profile of v2, /device:TPU:1, one launch (start us, length us, event | category | flops | bytes accessed | tf_op | source)
XLA Modules:
  0.0 34.0 jit_solution(6786865542737753997)
XLA Ops:
  0.0 32.5 %shard_map.109 = f32[2,32,256]{2,1,0:T(8,128)} custom-call(bf16[32,2,256]{2,1,0:T(2,128)(2,1)} %vec_h.1, s32[1,32]{1,0:T(1,128)} %bitcast.14, s32[1,32]{1,0:T(1,128)} %bitcast.15, s32[1,128]{1,0:T(1,128)} %bitcast.16, s32[1,128]{1,0:T(1,128)} %bitcast.17, bf16[32,256,256]{2,1,0:T(8,128)(2,1)} %self_h.1, bf16[32,256,256]{2,1,0:T(8,128)(2,1)} %near_h.1, ...), custom_call_target="tpu_custom_call" | custom-call | tf_op jit(solution)/shard_map/pallas_call | solution.py:454
  32.5 1.5 %copy.12 = f32[32,2,256]{2,1,0:T(2,128)} copy(f32[32,2,256]{2,0,1:T(8,128)} %bitcast.13) | data formatting | bytes 131072 | tf_op jit(solution)/shard_map/transpose | solution.py:504

commit v3 on v2

--- a/solution.py
+++ b/solution.py
@@ -141,8 +141,8 @@
     vec, near_row, near_col, far_row, far_col,
     selfs, nears, bases, trans, coup, roots,
     x32, xs, xn, cs, ps, fs, terms, sums, nearp, nwork, back, backin,
-    ga, gb, gc, gcin, nsend, nrecv,
-    load_sem, send_sem, a_recv, b_recv, c_recv, o_recv,
+    ga, gb, gc, gcin, nsend, nrecv, cnear, picked, partners, outgoing, incoming, halves, other,
+    load_sem, send_sem, a_recv, b_recv, c_recv, o_recv, seen, known,
 ):
     s = lax.axis_index("sub")
     y = lax.axis_index("lvl")
@@ -177,14 +177,7 @@
         return lax.div(m, 4), lax.rem(m, 4)
 
     barrier = pltpu.get_barrier_semaphore()
-    peers = [
-        at(i, j, k)
-        for i in range(4)
-        for j in range(4)
-        for k in range(4)
-        if 0 < (i > 0) + (j > 0) + (k > 0) < 3
-    ]
-    peers = peers + [sibling] + [shifted(o) for o in OFFSETS]
+    peers = [at(**{d: o}) for d in "xyz" for o in (1, 2, 3)] + [sibling]
     for peer in peers:
         pl.semaphore_signal(barrier, inc=1, device_id=peer, device_id_type=MESH)
 
@@ -204,46 +197,8 @@
             device_id=sibling, device_id_type=MESH,
         ).wait_recv()
 
-    class Stream:
-        def __init__(self, ref, order, rsem):
-            self.ref, self.rsem, self.dims = ref, rsem, order
-            self.f, self.s, self.t = (place[d] for d in order)
-
-        def behind(self, index, o):
-            return lax.rem(index + 4 - o, 4)
-
-        def spread(self):
-            mine = self.ref.at[c, self.t, self.s, self.f]
-            for i in (2, 1, 3, 0):
-                for j in (2, 1, 3, 0):
-                    if i or j:
-                        k = 4 * i + (j if i == 0 else 0)
-                        send(mine, mine, self.rsem.at[k], at(**{self.dims[1]: i, self.dims[0]: j}))
-
-        def relay(self, i):
-            if i == 0:
-                for j in (1, 2, 3):
-                    arrive(self.ref.at[c, self.t, self.s, self.behind(self.f, j)], self.rsem.at[j])
-            else:
-                arrive(self.ref.at[c, self.t, self.behind(self.s, i)], self.rsem.at[4 * i])
-            row = self.ref.at[c, self.t, self.behind(self.s, i)]
-            for o in (2, 1, 3):
-                send(row, row, self.rsem.at[16 + 4 * o + i], at(**{self.dims[2]: o}))
-
-        def take(self, o):
-            if o:
-                for i in range(4):
-                    arrive(self.ref.at[c, self.behind(self.t, o), self.behind(self.s, i)], self.rsem.at[16 + 4 * o + i])
-            plane = self.ref.at[c, self.behind(self.t, o)]
-            send(plane, plane, self.rsem.at[32 + o], sibling)
-            return c, self.behind(self.t, o)
-
-        def take_other(self, o):
-            arrive(self.ref.at[1 - c, self.behind(self.t, o)], self.rsem.at[32 + o])
-            return 1 - c, self.behind(self.t, o)
-
-    sa = Stream(ga, "yxz", a_recv)
-    sb = Stream(gb, "yzx", b_recv)
+    def back_by(index, o):
+        return lax.rem(index + 4 - o, 4)
 
     for i in range(5):
         loads[i].wait()
@@ -269,7 +224,7 @@
 
     lax.fori_loop(0, 4, coeff_group, 0)
     ch, cl = split(cs[...])
-    ga[c, z, x, y] = ch
+    ga[x, z, c] = ch
 
     terms[...] = tn(ch, own_hot) + tn(cl, own_hot)
     loads[6].wait()
@@ -282,7 +237,7 @@
     pos = nn(jnp.broadcast_to(is_far.astype(F32), (16, 128)).astype(BF16), before)[0:1, :].astype(jnp.int32)
     pos = jnp.where(is_far, pos, -1000)
     far_hot = (iota((32, 128), 0) == pos).astype(BF16)
-    gb[c, x, z, y] = nt(far_hot, bh).astype(BF16)
+    gb[x, y] = nt(far_hot, bh).astype(BF16)
     leaf_of = iota((32, 128), 0)
     near_hot = jnp.concatenate(
         [(leaf_of + ((me + o + 128) % 128) * 32 == far_c).astype(BF16) for o in OFFSETS], axis=0
@@ -301,13 +256,12 @@
     gcin[y] = tile.astype(BF16)
 
     pl.semaphore_wait(barrier, len(peers))
-    sa.spread()
-    sb.spread()
     for o in (1, 2, 3):
+        pl.semaphore_signal(seen, inc=1, device_id=at(x=o), device_id_type=MESH)
+    send(ga.at[x, z, c], ga.at[x, z, c], a_recv.at[0], sibling)
+    for o in (2, 1, 3):
         send(gcin.at[y], gcin.at[y], c_recv.at[o], at(y=o))
-    send(xs, xn, o_recv.at[0], shifted(-1))
-    for i, o in enumerate(OFFSETS):
-        send(nsend.at[i], nrecv.at[i], o_recv.at[2 + i], shifted(o))
+        send(gb.at[x, y], gb.at[x, y], b_recv.at[o], at(y=o))
 
     def run_blocks(src, dst, blocks, product):
         def body(g, carry):
@@ -321,6 +275,9 @@
 
         lax.fori_loop(0, 4, body, 0)
 
+    arrive(ga.at[x, z, 1 - c], a_recv.at[0])
+    for o in (2, 1, 3):
+        send(ga.at[x, z], ga.at[x, z], a_recv.at[o], at(z=o))
     loads[8].wait()
     run_blocks(x32, nearp, selfs, nt)
 
@@ -330,26 +287,77 @@
         nwork[v] = tn(row_hot, xs[v])
     loads[9].wait()
     run_blocks(nwork, nwork, nears, nn)
+
+    for o in (1, 3, 2):
+        arrive(gcin.at[back_by(y, o)], c_recv.at[o])
+    pl.semaphore_wait(seen, 3)
+    merged = gcin[0].astype(F32) + gcin[1].astype(F32) + gcin[2].astype(F32) + gcin[3].astype(F32)
+    gc[c, z, x] = merged.astype(BF16)
+    beside = [at(x=1), at(x=3), at(x=1, z=1), at(x=3, z=3)]
+    for peer in beside:
+        pl.semaphore_signal(known, inc=1, device_id=peer, device_id_type=MESH)
+    for i, j in ((0, 2), (0, 1), (0, 3), (2, 2), (2, 1), (2, 3), (1, 2), (3, 2), (1, 1), (1, 3), (3, 1), (3, 3), (2, 0), (1, 0), (3, 0)):
+        k = 4 + 4 * i + (j if i == 0 else 0)
+        send(gc.at[c, z, x], gc.at[c, z, x], c_recv.at[k], at(z=i, x=j))
+    for o in (1, 3, 2):
+        arrive(gb.at[x, back_by(y, o)], b_recv.at[o])
+    for o in (2, 1, 3):
+        send(gb.at[x], gb.at[x], b_recv.at[3 + o], at(x=o))
+
+    def decode(t):
+        d = t[0:1, :].astype(jnp.int32)
+        return d % 4, d // 32, (d // 8) % 4, (d // 4) % 2, t[1:2, :].astype(jnp.int32)
+
+    ty, tz, tx, tc, tleaf = decode(merged)
+    slot = jnp.where(ty == y, ((tx * 4 + tz) * 2 + tc) * 32 + tleaf, -1).astype(F32)
+    slots = jnp.transpose(jnp.broadcast_to(slot, (128, 128)))
+    slot_hot = jnp.concatenate(
+        [(slots == (iota((128, 128), 1) + 128 * i).astype(F32)).astype(BF16) for i in range(8)], axis=1
+    )
+
     for v in range(2):
         both = pick(col_hot, nwork[v])
         nearp[v] = nearp[v] + both[0:32]
         back[v] = both[32:64]
+
+    for o in (1, 3, 2):
+        arrive(ga.at[x, back_by(z, o)], a_recv.at[o])
+    for o in (2, 1, 3):
+        send(ga.at[x], ga.at[x], a_recv.at[3 + o], at(x=o))
+
+    pl.semaphore_wait(known, len(beside))
+    send(xs, xn, o_recv.at[0], shifted(-1))
+    for i, o in enumerate(OFFSETS):
+        send(ga.at[x, z, c], cnear.at[5 - i], o_recv.at[13 - i], shifted(o))
+    for i, o in enumerate(OFFSETS):
+        send(nsend.at[i], nrecv.at[i], o_recv.at[2 + i], shifted(o))
     send(back, backin, o_recv.at[1], shifted(1))
 
-    sa.relay(0)
-    sb.relay(0)
-    for o in (1, 2, 3):
-        arrive(gcin.at[lax.rem(y + 4 - o, 4)], c_recv.at[o])
-    merged = gcin[0].astype(F32) + gcin[1].astype(F32) + gcin[2].astype(F32) + gcin[3].astype(F32)
-    gc[c, z, x] = merged.astype(BF16)
-    for i in (2, 1, 3, 0):
-        for j in (2, 1, 3, 0):
-            if i or j:
-                k = 4 + 4 * i + (j if i == 0 else 0)
-                send(gc.at[c, z, x], gc.at[c, z, x], c_recv.at[k], at(z=i, x=j))
+    for j in (1, 3, 2):
+        arrive(gc.at[c, z, back_by(x, j)], c_recv.at[4 + j])
+        arrive(gb.at[back_by(x, j)], b_recv.at[3 + j])
+    hots = []
+    for j in range(4):
+        ty, tz, tx, tc, tleaf = decode(gc[c, z, j].astype(F32))
+        line = jnp.where((ty == y) & (tx == x), (tz * 2 + tc) * 32 + tleaf, -1)
+        hots.append((iota((256, 128), 0) == line).astype(F32).astype(BF16))
+    outgoing[...] = nn(jnp.concatenate(hots, axis=1), gb[...].reshape(512, 128)).reshape(4, 64, 128)
+    for o in (2, 1, 3):
+        to = lax.rem(z + o, 4)
+        send(outgoing.at[to], incoming.at[z], b_recv.at[6 + o], at(z=o))
+    incoming[z] = outgoing[z]
+
+    for o in (1, 3, 2):
+        arrive(ga.at[back_by(x, o)], a_recv.at[3 + o])
+    picked[...] = nn(slot_hot, ga[...].reshape(1024, 128)).astype(BF16).reshape(4, 32, 128)
+    for o in (2, 1, 3):
+        to = lax.rem(y + o, 4)
+        send(picked.at[to], partners.at[y], a_recv.at[6 + o], at(y=o))
+    partners[y] = picked[y]
+
     for i in (1, 3, 2):
-        sa.relay(i)
-        sb.relay(i)
+        arrive(gc.at[c, back_by(z, i)], c_recv.at[4 + 4 * i])
+    send(gc.at[c], gc.at[c], c_recv.at[0], sibling)
 
     arrive(xn, o_recv.at[0])
     for v in range(2):
@@ -357,34 +365,6 @@
     run_blocks(nwork, nwork, nears, nt)
     for v in range(2):
         nearp[v] = nearp[v] + pick(row_hot, nwork[v])
-
-    ldev = far_c // 32
-    perm = ((ldev // 4) % 2) * 64 + (ldev // 32) * 16 + ((ldev // 8) % 4) * 4 + ldev % 4
-    code = (perm * 32 + far_c - ldev * 32).astype(F32)
-    codes_q = jnp.transpose(jnp.broadcast_to(code, (128, 128)))
-    lane = iota((128, 128), 1).astype(F32)
-
-    def gather(place_a, partner):
-        i, j = place_a
-        for k in range(4):
-            base = (((i * 4 + j) * 4 + k) * 128).astype(F32)
-            partner = partner + nn((codes_q == lane + base).astype(BF16), ga[i, j, k].reshape(128, 128))
-        return partner
-
-    sa.take(0)
-    sb.take(0)
-    for i in range(4):
-        if i:
-            arrive(gc.at[c, lax.rem(z + 4 - i, 4)], c_recv.at[4 + 4 * i])
-        else:
-            for j in (1, 2, 3):
-                arrive(gc.at[c, z, lax.rem(x + 4 - j, 4)], c_recv.at[4 + j])
-    send(gc.at[c], gc.at[c], c_recv.at[0], sibling)
-    partner = gather((c, z), jnp.zeros((128, 128), F32))
-    for o in (1, 3, 2):
-        where = sa.take(o)
-        sb.take(o)
-        partner = gather(where, partner)
 
     arrive(gc.at[1 - c], c_recv.at[0])
     row_at = iota((128, 512), 1)
@@ -403,28 +383,28 @@
     fs[1, 0:8, :] = d1
     tree_down(fs, trans)
 
-    for o in (0, 1, 3, 2):
-        partner = gather(sa.take_other(o), partner)
-    terms[...] = jnp.transpose(partner)
-    contract(coup, terms, sums)
-    sh, sl = split(sums[...])
-    acc = nt(own_hot, sh) + nt(own_hot, sl)
-
-    def deliver(place_b, acc):
-        i, j = place_b
-        for k in range(4):
-            t = gc[i, k, j].astype(F32)
-            hot = ((t[0:1, :] == me.astype(F32)) & (t[1:2, :] == leaf_of.astype(F32))).astype(BF16)
-            acc = acc + nn(hot, gb[i, j, k].reshape(128, 128))
-        return acc
-
-    for o in range(4):
-        acc = deliver((c, lax.rem(x + 4 - o, 4)), acc)
+    for o in (1, 3, 2):
+        arrive(incoming.at[back_by(z, o)], b_recv.at[6 + o])
+    total = incoming[0] + incoming[1] + incoming[2] + incoming[3]
+    halves[0] = total[0:32]
+    halves[1] = total[32:64]
+    send(halves.at[1 - c], other, b_recv.at[0], sibling)
+    for i in range(6):
+        arrive(cnear.at[i], o_recv.at[8 + i])
+    near_terms = tn(cnear[...].reshape(192, 128), near_hot)
+    acc = halves[c]
     for i in range(6):
         arrive(nrecv.at[i], o_recv.at[2 + i])
         acc = acc + nrecv[i].astype(F32)
-    for o in (0, 1, 3, 2):
-        acc = deliver(sb.take_other(o), acc)
+    for o in (1, 3, 2):
+        arrive(partners.at[back_by(y, o)], a_recv.at[6 + o])
+    rows = partners[0].astype(F32) + partners[1].astype(F32) + partners[2].astype(F32) + partners[3].astype(F32)
+    terms[...] = near_terms + tn(rows.astype(BF16), far_hot)
+    contract(coup, terms, sums)
+    sh, sl = split(sums[...])
+    acc = acc + nt(own_hot, sh) + nt(own_hot, sl)
+    arrive(other, b_recv.at[0])
+    acc = acc + other[...]
 
     field = acc + jnp.where(iota((32, 128), 1) < 64, fs[0], fs[1])
     d0, d1 = doubled(field.astype(BF16).astype(F32))
@@ -480,18 +460,27 @@
             pltpu.VMEM((2, 32, 256), F32),
             pltpu.VMEM((2, 32, 256), F32),
             pltpu.VMEM((2, 32, 256), F32),
-            pltpu.VMEM((2, 4, 4, 4, 32, 128), BF16),
-            pltpu.VMEM((2, 4, 4, 4, 32, 128), BF16),
+            pltpu.VMEM((4, 4, 2, 32, 128), BF16),
+            pltpu.VMEM((4, 4, 32, 128), BF16),
             pltpu.VMEM((2, 4, 4, 16, 128), BF16),
             pltpu.VMEM((4, 16, 128), BF16),
             pltpu.VMEM((6, 32, 128), BF16),
             pltpu.VMEM((6, 32, 128), BF16),
+            pltpu.VMEM((6, 32, 128), BF16),
+            pltpu.VMEM((4, 32, 128), BF16),
+            pltpu.VMEM((4, 32, 128), BF16),
+            pltpu.VMEM((4, 64, 128), F32),
+            pltpu.VMEM((4, 64, 128), F32),
+            pltpu.VMEM((2, 32, 128), F32),
+            pltpu.VMEM((32, 128), F32),
             pltpu.SemaphoreType.DMA((11,)),
             pltpu.SemaphoreType.DMA((104,)),
-            pltpu.SemaphoreType.DMA((36,)),
-            pltpu.SemaphoreType.DMA((36,)),
+            pltpu.SemaphoreType.DMA((10,)),
+            pltpu.SemaphoreType.DMA((10,)),
             pltpu.SemaphoreType.DMA((20,)),
-            pltpu.SemaphoreType.DMA((8,)),
+            pltpu.SemaphoreType.DMA((14,)),
+            pltpu.SemaphoreType.REGULAR,
+            pltpu.SemaphoreType.REGULAR,
         ],
         compiler_params=pltpu.CompilerParams(
             collective_id=0, has_side_effects=True, vmem_limit_bytes=62 * 1024 * 1024

time: 34.2 us -> 29.9 us (0.87)
  Pallas kernels: 32.5 us -> 28.3 us
    pallas_call x1, Pallas kernels: 32.5 us -> 28.3 us  [shards(): pl.pallas_call(kernel, out_shape=jax.ShapeDtypeStruct((2, 32, 256), F32),...]
where the time goes in v3:
time: 29.9 us; the launch traced here: 29.8 us
  Pallas kernels  28.3 us (95%)
  local copies, waits for them, and re-layouts  1.52 us (5%)
    pallas_call x1, Pallas kernels, shards(): pl.pallas_call(kernel, out_shape=jax.ShapeDtypeStruct((2, 32, 256), F32),...  28.3 us
    transpose x1, local copies, waits for them, and re-layouts, shards(): return result.transpose(1, 0, 2)  1.52 us

profile of v3, /device:TPU:1, one launch (start us, length us, event | category | flops | bytes accessed | tf_op | source)
XLA Modules:
  0.0 29.8 jit_solution(9901903224520083584)
XLA Ops:
  0.0 28.3 %shard_map.109 = f32[2,32,256]{2,1,0:T(8,128)} custom-call(bf16[32,2,256]{2,1,0:T(2,128)(2,1)} %vec_h.1, s32[1,32]{1,0:T(1,128)} %bitcast.14, s32[1,32]{1,0:T(1,128)} %bitcast.15, s32[1,128]{1,0:T(1,128)} %bitcast.16, s32[1,128]{1,0:T(1,128)} %bitcast.17, bf16[32,256,256]{2,1,0:T(8,128)(2,1)} %self_h.1, bf16[32,256,256]{2,1,0:T(8,128)(2,1)} %near_h.1, ...), custom_call_target="tpu_custom_call" | custom-call | tf_op jit(solution)/shard_map/pallas_call | solution.py:434
  28.3 1.5 %copy.12 = f32[32,2,256]{2,1,0:T(2,128)} copy(f32[32,2,256]{2,0,1:T(8,128)} %bitcast.13) | data formatting | bytes 131072 | tf_op jit(solution)/shard_map/transpose | solution.py:493

commit v4 on v3

--- a/solution.py
+++ b/solution.py
@@ -115,16 +115,18 @@
         cs[0:half, :] = ps[pl.ds(0, half, stride=2), :] + ps[pl.ds(1, half, stride=2), :]
 
 
-def tree_down(fs, trans):
+def tree_down(fs, halved):
     for offset, width in reversed(LEVELS):
         count = min(width, 8)
         groups = []
         for g in range(width // count):
             f = jnp.concatenate([fs[0, 8 * g : 8 * g + 8, :], fs[1, 8 * g : 8 * g + 8, :]], axis=0)
             fh, fl = split(f[:, 0:64])
-            e = trans[offset + 8 * g : offset + 8 * g + count].reshape(64 * count, 64)
-            eh, el = split(e)
-            groups.append(collect(nt(fh, eh) + nt(fl, eh) + nt(fh, el), count))
+            here = slice(offset + 8 * g, offset + 8 * g + count)
+            eh = halved[0, here].reshape(64 * count, 64)
+            el = halved[1, here].reshape(64 * count, 64)
+            main = nt(jnp.concatenate([fh, fl], axis=0), eh)
+            groups.append(collect(main[0:16] + main[16:32] + nt(fh, el), count))
         for g, child in enumerate(groups):
             for v in range(2):
                 if offset == 0:
@@ -140,8 +142,8 @@
     out,
     vec, near_row, near_col, far_row, far_col,
     selfs, nears, bases, trans, coup, roots,
-    x32, xs, xn, cs, ps, fs, terms, sums, nearp, nwork, back, backin,
-    ga, gb, gc, gcin, nsend, nrecv, cnear, picked, partners, outgoing, incoming, halves, other,
+    halved, x32, xs, xn, cs, ps, fs, terms, sums, nearp, nwork, back, backin,
+    ga, gb, gc, gcin, gq, gqin, nsend, nrecv, cnear, picked, partners, outgoing, incoming, halves, other,
     load_sem, send_sem, a_recv, b_recv, c_recv, o_recv, seen, known,
 ):
     s = lax.axis_index("sub")
@@ -224,7 +226,7 @@
 
     lax.fori_loop(0, 4, coeff_group, 0)
     ch, cl = split(cs[...])
-    ga[x, z, c] = ch
+    ga[z, x, c] = ch
 
     terms[...] = tn(ch, own_hot) + tn(cl, own_hot)
     loads[6].wait()
@@ -238,6 +240,26 @@
     pos = jnp.where(is_far, pos, -1000)
     far_hot = (iota((32, 128), 0) == pos).astype(BF16)
     gb[x, y] = nt(far_hot, bh).astype(BF16)
+    lane_hot = (iota((128, 128), 0) == pos + 32 * y).astype(BF16)
+    row_id = iota((16, 128), 0)
+    codes = jnp.where(row_id == 0, dev, jnp.where(row_id == 1, far_c - dev * 32, 0)).astype(F32).astype(BF16)
+    gqin[y] = nt(codes, lane_hot).astype(BF16)
+    pl.semaphore_wait(barrier, len(peers))
+    send(ga.at[z, x, c], ga.at[z, x, c], a_recv.at[0], sibling)
+    for o in (1, 2, 3):
+        pl.semaphore_signal(seen, inc=1, device_id=at(x=o), device_id_type=MESH)
+        pl.semaphore_signal(seen, inc=1, device_id=at(y=o), device_id_type=MESH)
+    for o in (2, 1, 3):
+        send(gqin.at[y], gqin.at[y], c_recv.at[16 + o], at(y=o))
+        send(gb.at[x, y], gb.at[x, y], b_recv.at[o], at(y=o))
+
+    arrive(ga.at[z, x, 1 - c], a_recv.at[0])
+    for o in (2, 1, 3):
+        send(ga.at[z, x], ga.at[z, x], a_recv.at[o], at(x=o))
+    for o in (2, 1, 3):
+        send(ga.at[z, x], ga.at[z, x], a_recv.at[3 + o], at(z=o))
+        send(gb.at[x, y], gb.at[x, y], b_recv.at[3 + o], at(x=o))
+
     leaf_of = iota((32, 128), 0)
     near_hot = jnp.concatenate(
         [(leaf_of + ((me + o + 128) % 128) * 32 == far_c).astype(BF16) for o in OFFSETS], axis=0
@@ -247,21 +269,15 @@
     loads[7].wait()
     tree_up(cs, ps, trans)
     rh, rl = split(cs[0:1, :])
-    lane_hot = (iota((128, 128), 0) == pos + 32 * y).astype(BF16)
-    row_id = iota((16, 128), 0)
-    codes = jnp.where(row_id == 0, dev, jnp.where(row_id == 1, far_c - dev * 32, 0)).astype(F32).astype(BF16)
-    tile = nt(codes, lane_hot)
-    tile = jnp.where(row_id == 4 + 2 * y, rh.astype(F32), tile)
-    tile = jnp.where(row_id == 5 + 2 * y, rl.astype(F32), tile)
+    tile = jnp.where(row_id == 4 + 2 * y, rh.astype(F32), jnp.where(row_id == 5 + 2 * y, rl.astype(F32), 0.0))
     gcin[y] = tile.astype(BF16)
-
-    pl.semaphore_wait(barrier, len(peers))
-    for o in (1, 2, 3):
-        pl.semaphore_signal(seen, inc=1, device_id=at(x=o), device_id_type=MESH)
-    send(ga.at[x, z, c], ga.at[x, z, c], a_recv.at[0], sibling)
     for o in (2, 1, 3):
         send(gcin.at[y], gcin.at[y], c_recv.at[o], at(y=o))
-        send(gb.at[x, y], gb.at[x, y], b_recv.at[o], at(y=o))
+
+    pl.semaphore_wait(seen, 6)
+    beside = [at(x=1), at(x=3), at(x=1, z=1), at(x=3, z=3)]
+    for peer in beside:
+        pl.semaphore_signal(known, inc=1, device_id=peer, device_id_type=MESH)
 
     def run_blocks(src, dst, blocks, product):
         def body(g, carry):
@@ -275,11 +291,40 @@
 
         lax.fori_loop(0, 4, body, 0)
 
-    arrive(ga.at[x, z, 1 - c], a_recv.at[0])
-    for o in (2, 1, 3):
-        send(ga.at[x, z], ga.at[x, z], a_recv.at[o], at(z=o))
     loads[8].wait()
     run_blocks(x32, nearp, selfs, nt)
+
+    for o in (1, 3, 2):
+        block = ga.at[z, back_by(x, o)]
+        arrive(block, a_recv.at[o])
+        for p in (2, 1, 3):
+            send(block, block, a_recv.at[3 + p], at(z=p))
+    for o in (1, 3, 2):
+        block = gb.at[x, back_by(y, o)]
+        arrive(gqin.at[back_by(y, o)], c_recv.at[16 + o])
+        arrive(block, b_recv.at[o])
+        for p in (2, 1, 3):
+            send(block, block, b_recv.at[3 + p], at(x=p))
+    merged = gqin[0].astype(F32) + gqin[1].astype(F32) + gqin[2].astype(F32) + gqin[3].astype(F32)
+    gq[x] = merged.astype(BF16)
+    for o in (2, 1, 3):
+        send(gq.at[x], gq.at[x], c_recv.at[19 + o], at(x=o))
+
+    for o in (1, 3, 2):
+        arrive(gcin.at[back_by(y, o)], c_recv.at[o])
+    gc[c, z, x] = (
+        gcin[0].astype(F32) + gcin[1].astype(F32) + gcin[2].astype(F32) + gcin[3].astype(F32)
+    ).astype(BF16)
+    for i, j in ((2, 2), (2, 1), (2, 3), (1, 2), (3, 2), (1, 1), (1, 3), (3, 1), (3, 3), (0, 2), (2, 0), (0, 1), (0, 3), (1, 0), (3, 0)):
+        k = 4 + 4 * i + (j if i == 0 else 0)
+        send(gc.at[c, z, x], gc.at[c, z, x], c_recv.at[k], at(z=i, x=j))
+
+    pl.semaphore_wait(known, len(beside))
+    send(xs, xn, o_recv.at[0], shifted(-1))
+    for i, o in enumerate(OFFSETS):
+        send(ga.at[z, x, c], cnear.at[5 - i], o_recv.at[13 - i], shifted(o))
+    for i, o in enumerate(OFFSETS):
+        send(nsend.at[i], nrecv.at[i], o_recv.at[2 + i], shifted(o))
 
     row_hot = (iota((32, 32), 0) == near_row[...]).astype(BF16)
     col_hot = (iota((64, 32), 0) == near_col[...]).astype(BF16)
@@ -288,57 +333,30 @@
     loads[9].wait()
     run_blocks(nwork, nwork, nears, nn)
 
-    for o in (1, 3, 2):
-        arrive(gcin.at[back_by(y, o)], c_recv.at[o])
-    pl.semaphore_wait(seen, 3)
-    merged = gcin[0].astype(F32) + gcin[1].astype(F32) + gcin[2].astype(F32) + gcin[3].astype(F32)
-    gc[c, z, x] = merged.astype(BF16)
-    beside = [at(x=1), at(x=3), at(x=1, z=1), at(x=3, z=3)]
-    for peer in beside:
-        pl.semaphore_signal(known, inc=1, device_id=peer, device_id_type=MESH)
-    for i, j in ((0, 2), (0, 1), (0, 3), (2, 2), (2, 1), (2, 3), (1, 2), (3, 2), (1, 1), (1, 3), (3, 1), (3, 3), (2, 0), (1, 0), (3, 0)):
-        k = 4 + 4 * i + (j if i == 0 else 0)
-        send(gc.at[c, z, x], gc.at[c, z, x], c_recv.at[k], at(z=i, x=j))
-    for o in (1, 3, 2):
-        arrive(gb.at[x, back_by(y, o)], b_recv.at[o])
-    for o in (2, 1, 3):
-        send(gb.at[x], gb.at[x], b_recv.at[3 + o], at(x=o))
+    for v in range(2):
+        both = pick(col_hot, nwork[v])
+        nearp[v] = nearp[v] + both[0:32]
+        back[v] = both[32:64]
+
+    send(back, backin, o_recv.at[1], shifted(1))
 
     def decode(t):
         d = t[0:1, :].astype(jnp.int32)
         return d % 4, d // 32, (d // 8) % 4, (d // 4) % 2, t[1:2, :].astype(jnp.int32)
 
     ty, tz, tx, tc, tleaf = decode(merged)
-    slot = jnp.where(ty == y, ((tx * 4 + tz) * 2 + tc) * 32 + tleaf, -1).astype(F32)
+    slot = jnp.where(ty == y, ((tz * 4 + tx) * 2 + tc) * 32 + tleaf, -1).astype(F32)
     slots = jnp.transpose(jnp.broadcast_to(slot, (128, 128)))
     slot_hot = jnp.concatenate(
         [(slots == (iota((128, 128), 1) + 128 * i).astype(F32)).astype(BF16) for i in range(8)], axis=1
     )
 
-    for v in range(2):
-        both = pick(col_hot, nwork[v])
-        nearp[v] = nearp[v] + both[0:32]
-        back[v] = both[32:64]
-
-    for o in (1, 3, 2):
-        arrive(ga.at[x, back_by(z, o)], a_recv.at[o])
-    for o in (2, 1, 3):
-        send(ga.at[x], ga.at[x], a_recv.at[3 + o], at(x=o))
-
-    pl.semaphore_wait(known, len(beside))
-    send(xs, xn, o_recv.at[0], shifted(-1))
-    for i, o in enumerate(OFFSETS):
-        send(ga.at[x, z, c], cnear.at[5 - i], o_recv.at[13 - i], shifted(o))
-    for i, o in enumerate(OFFSETS):
-        send(nsend.at[i], nrecv.at[i], o_recv.at[2 + i], shifted(o))
-    send(back, backin, o_recv.at[1], shifted(1))
-
     for j in (1, 3, 2):
-        arrive(gc.at[c, z, back_by(x, j)], c_recv.at[4 + j])
+        arrive(gq.at[back_by(x, j)], c_recv.at[19 + j])
         arrive(gb.at[back_by(x, j)], b_recv.at[3 + j])
     hots = []
     for j in range(4):
-        ty, tz, tx, tc, tleaf = decode(gc[c, z, j].astype(F32))
+        ty, tz, tx, tc, tleaf = decode(gq[j].astype(F32))
         line = jnp.where((ty == y) & (tx == x), (tz * 2 + tc) * 32 + tleaf, -1)
         hots.append((iota((256, 128), 0) == line).astype(F32).astype(BF16))
     outgoing[...] = nn(jnp.concatenate(hots, axis=1), gb[...].reshape(512, 128)).reshape(4, 64, 128)
@@ -348,13 +366,27 @@
     incoming[z] = outgoing[z]
 
     for o in (1, 3, 2):
-        arrive(ga.at[back_by(x, o)], a_recv.at[3 + o])
+        arrive(ga.at[back_by(z, o)], a_recv.at[3 + o])
     picked[...] = nn(slot_hot, ga[...].reshape(1024, 128)).astype(BF16).reshape(4, 32, 128)
     for o in (2, 1, 3):
         to = lax.rem(y + o, 4)
         send(picked.at[to], partners.at[y], a_recv.at[6 + o], at(y=o))
     partners[y] = picked[y]
 
+    def halve(i, carry):
+        hi, lo = split(trans[pl.ds(2 * i, 2)])
+        halved[0, pl.ds(2 * i, 2)] = hi
+        halved[1, pl.ds(2 * i, 2)] = lo
+        return carry
+
+    lax.fori_loop(0, 31, halve, 0)
+    row_at = iota((128, 512), 1)
+    tile_at = row_at // 16
+    line = row_at % 16
+    holder = (((tile_at // 4) % 4 * 4 + tile_at % 4) * 2 + tile_at // 16) * 4 + (line - 4) // 2
+    sel = ((holder == iota((128, 512), 0)) & (line >= 4) & (line < 12)).astype(BF16)
+    for j in (1, 3, 2):
+        arrive(gc.at[c, z, back_by(x, j)], c_recv.at[4 + j])
     for i in (1, 3, 2):
         arrive(gc.at[c, back_by(z, i)], c_recv.at[4 + 4 * i])
     send(gc.at[c], gc.at[c], c_recv.at[0], sibling)
@@ -365,23 +397,6 @@
     run_blocks(nwork, nwork, nears, nt)
     for v in range(2):
         nearp[v] = nearp[v] + pick(row_hot, nwork[v])
-
-    arrive(gc.at[1 - c], c_recv.at[0])
-    row_at = iota((128, 512), 1)
-    tile_at = row_at // 16
-    line = row_at % 16
-    holder = (((tile_at // 4) % 4 * 4 + tile_at % 4) * 2 + tile_at // 16) * 4 + (line - 4) // 2
-    sel = ((holder == iota((128, 512), 0)) & (line >= 4) & (line < 12)).astype(BF16)
-    terms[...] = jnp.transpose(nn(sel, gc[...].reshape(512, 128)))
-    loads[10].wait()
-    contract(roots, terms, sums)
-    sh, sl = split(sums[...])
-    ones = jnp.ones((16, 128), BF16)
-    top = (nt(ones, sh) + nt(ones, sl))[0:8]
-    d0, d1 = doubled(top)
-    fs[0, 0:8, :] = d0
-    fs[1, 0:8, :] = d1
-    tree_down(fs, trans)
 
     for o in (1, 3, 2):
         arrive(incoming.at[back_by(z, o)], b_recv.at[6 + o])
@@ -396,6 +411,19 @@
     for i in range(6):
         arrive(nrecv.at[i], o_recv.at[2 + i])
         acc = acc + nrecv[i].astype(F32)
+
+    arrive(gc.at[1 - c], c_recv.at[0])
+    terms[...] = jnp.transpose(nn(sel, gc[...].reshape(512, 128)))
+    loads[10].wait()
+    contract(roots, terms, sums)
+    sh, sl = split(sums[...])
+    ones = jnp.ones((16, 128), BF16)
+    top = (nt(ones, sh) + nt(ones, sl))[0:8]
+    d0, d1 = doubled(top)
+    fs[0, 0:8, :] = d0
+    fs[1, 0:8, :] = d1
+    tree_down(fs, halved)
+
     for o in (1, 3, 2):
         arrive(partners.at[back_by(y, o)], a_recv.at[6 + o])
     rows = partners[0].astype(F32) + partners[1].astype(F32) + partners[2].astype(F32) + partners[3].astype(F32)
@@ -448,6 +476,7 @@
             pltpu.VMEM((62, 64, 64), F32),
             pltpu.VMEM((64, 64, 128), F32),
             pltpu.VMEM((64, 64, 128), F32),
+            pltpu.VMEM((2, 62, 64, 64), BF16),
             pltpu.VMEM((2, 32, 256), F32),
             pltpu.VMEM((2, 32, 256), BF16),
             pltpu.VMEM((2, 32, 256), BF16),
@@ -464,6 +493,8 @@
             pltpu.VMEM((4, 4, 32, 128), BF16),
             pltpu.VMEM((2, 4, 4, 16, 128), BF16),
             pltpu.VMEM((4, 16, 128), BF16),
+            pltpu.VMEM((4, 16, 128), BF16),
+            pltpu.VMEM((4, 16, 128), BF16),
             pltpu.VMEM((6, 32, 128), BF16),
             pltpu.VMEM((6, 32, 128), BF16),
             pltpu.VMEM((6, 32, 128), BF16),
@@ -477,7 +508,7 @@
             pltpu.SemaphoreType.DMA((104,)),
             pltpu.SemaphoreType.DMA((10,)),
             pltpu.SemaphoreType.DMA((10,)),
-            pltpu.SemaphoreType.DMA((20,)),
+            pltpu.SemaphoreType.DMA((23,)),
             pltpu.SemaphoreType.DMA((14,)),
             pltpu.SemaphoreType.REGULAR,
             pltpu.SemaphoreType.REGULAR,

time: 29.9 us -> 29 us (0.970)
  Pallas kernels: 28.3 us -> 27.3 us
    pallas_call x1, Pallas kernels: 28.3 us -> 27.3 us  [shards(): pl.pallas_call(kernel, out_shape=jax.ShapeDtypeStruct((2, 32, 256), F32),...]
where the time goes in v4:
time: 29 us; the launch traced here: 28.8 us
  Pallas kernels  27.3 us (94%)
  local copies, waits for them, and re-layouts  1.52 us (5%)
    pallas_call x1, Pallas kernels, shards(): pl.pallas_call(kernel, out_shape=jax.ShapeDtypeStruct((2, 32, 256), F32),...  27.3 us
    transpose x1, local copies, waits for them, and re-layouts, shards(): return result.transpose(1, 0, 2)  1.52 us

profile of v4, /device:TPU:1, one launch (start us, length us, event | category | flops | bytes accessed | tf_op | source)
XLA Modules:
  0.0 28.8 jit_solution(14991689914869631819)
XLA Ops:
  0.0 27.3 %shard_map.109 = f32[2,32,256]{2,1,0:T(8,128)} custom-call(bf16[32,2,256]{2,1,0:T(2,128)(2,1)} %vec_h.1, s32[1,32]{1,0:T(1,128)} %bitcast.14, s32[1,32]{1,0:T(1,128)} %bitcast.15, s32[1,128]{1,0:T(1,128)} %bitcast.16, s32[1,128]{1,0:T(1,128)} %bitcast.17, bf16[32,256,256]{2,1,0:T(8,128)(2,1)} %self_h.1, bf16[32,256,256]{2,1,0:T(8,128)(2,1)} %near_h.1, ...), custom_call_target="tpu_custom_call" | custom-call | tf_op jit(solution)/shard_map/pallas_call | solution.py:462
  27.3 1.5 %copy.12 = f32[32,2,256]{2,1,0:T(2,128)} copy(f32[32,2,256]{2,0,1:T(8,128)} %bitcast.13) | data formatting | bytes 131072 | tf_op jit(solution)/shard_map/transpose | solution.py:524

commit v5 on v4

--- a/solution.py
+++ b/solution.py
@@ -153,6 +153,25 @@
     c = lax.rem(s, 2)
     me = s * 4 + y
 
+    def at(x=0, y=0, z=0):
+        ox, oy, oz = x, y, z
+        return (
+            (lax.rem(place["z"] + oz, 4) * 4 + lax.rem(place["x"] + ox, 4)) * 2 + c,
+            lax.rem(place["y"] + oy, 4),
+        )
+
+    place = {"x": x, "y": y, "z": z}
+    sibling = ((z * 4 + x) * 2 + 1 - c, y)
+
+    def shifted(o):
+        m = lax.rem(me + o + 128, 128)
+        return lax.div(m, 4), lax.rem(m, 4)
+
+    barrier = pltpu.get_barrier_semaphore()
+    peers = [at(**{d: o}) for d in "xyz" for o in (1, 2, 3)] + [sibling]
+    for peer in peers:
+        pl.semaphore_signal(barrier, inc=1, device_id=peer, device_id_type=MESH)
+
     loads = []
     for i, (src, dst) in enumerate(
         (
@@ -164,25 +183,6 @@
         load.start()
         loads.append(load)
 
-    def at(x=0, y=0, z=0):
-        ox, oy, oz = x, y, z
-        return (
-            (lax.rem(place["z"] + oz, 4) * 4 + lax.rem(place["x"] + ox, 4)) * 2 + c,
-            lax.rem(place["y"] + oy, 4),
-        )
-
-    place = {"x": x, "y": y, "z": z}
-    sibling = ((z * 4 + x) * 2 + 1 - c, y)
-
-    def shifted(o):
-        m = lax.rem(me + o + 128, 128)
-        return lax.div(m, 4), lax.rem(m, 4)
-
-    barrier = pltpu.get_barrier_semaphore()
-    peers = [at(**{d: o}) for d in "xyz" for o in (1, 2, 3)] + [sibling]
-    for peer in peers:
-        pl.semaphore_signal(barrier, inc=1, device_id=peer, device_id_type=MESH)
-
     pending = []
 
     def send(src, dst, rsem, peer):
@@ -224,7 +224,7 @@
         cs[pl.ds(8 * g, 8), :] = abreast(collect(wide, 8))
         return carry
 
-    lax.fori_loop(0, 4, coeff_group, 0)
+    lax.fori_loop(0, 4, coeff_group, 0, unroll=True)
     ch, cl = split(cs[...])
     ga[z, x, c] = ch
 
@@ -289,7 +289,7 @@
                 dst[v, pl.ds(8 * g, 8), :] = acc[8 * v : 8 * v + 8]
             return carry
 
-        lax.fori_loop(0, 4, body, 0)
+        lax.fori_loop(0, 4, body, 0, unroll=True)
 
     loads[8].wait()
     run_blocks(x32, nearp, selfs, nt)
@@ -448,7 +448,7 @@
             out[v, here, :] = acc[8 * v : 8 * v + 8] + nearp[v, here, :] + backin[v, here, :]
         return carry
 
-    lax.fori_loop(0, 4, out_group, 0)
+    lax.fori_loop(0, 4, out_group, 0, unroll=True)
     for copy in pending:
         copy.wait_send()
 

time: 29 us -> 27.9 us (0.962)
  Pallas kernels: 27.3 us -> 26.3 us
    pallas_call x1, Pallas kernels: 27.3 us -> 26.3 us  [shards(): pl.pallas_call(kernel, out_shape=jax.ShapeDtypeStruct((2, 32, 256), F32),...]
where the time goes in v5:
time: 27.9 us; the launch traced here: 27.8 us
  Pallas kernels  26.3 us (94%)
  local copies, waits for them, and re-layouts  1.52 us (5%)
    pallas_call x1, Pallas kernels, shards(): pl.pallas_call(kernel, out_shape=jax.ShapeDtypeStruct((2, 32, 256), F32),...  26.3 us
    transpose x1, local copies, waits for them, and re-layouts, shards(): return result.transpose(1, 0, 2)  1.52 us

profile of v5, /device:TPU:1, one launch (start us, length us, event | category | flops | bytes accessed | tf_op | source)
XLA Modules:
  0.0 27.8 jit_solution(17161295985939239600)
XLA Ops:
  0.0 26.3 %shard_map.109 = f32[2,32,256]{2,1,0:T(8,128)} custom-call(bf16[32,2,256]{2,1,0:T(2,128)(2,1)} %vec_h.1, s32[1,32]{1,0:T(1,128)} %bitcast.14, s32[1,32]{1,0:T(1,128)} %bitcast.15, s32[1,128]{1,0:T(1,128)} %bitcast.16, s32[1,128]{1,0:T(1,128)} %bitcast.17, bf16[32,256,256]{2,1,0:T(8,128)(2,1)} %self_h.1, bf16[32,256,256]{2,1,0:T(8,128)(2,1)} %near_h.1, ...), custom_call_target="tpu_custom_call" | custom-call | tf_op jit(solution)/shard_map/pallas_call | solution.py:462
  26.3 1.5 %copy.12 = f32[32,2,256]{2,1,0:T(2,128)} copy(f32[32,2,256]{2,0,1:T(8,128)} %bitcast.13) | data formatting | bytes 131072 | tf_op jit(solution)/shard_map/transpose | solution.py:524
